TPU v7x, 256 devices: a whole 4x4x8 slice. The times are simulated.
256 devices in a mesh: dp: 16 (over z, core), seq: 16 (over y, x).
Axes of the slice: x: 4, y: 4, z: 8, core: 2. Of those that a mesh axis runs over, the one named last changes fastest.
Arguments:
- tokens: bfloat16 [32768, 2560], P(('dp', 'seq')), may hold values from -6 to 6
- modulation: float32 [4, 128, 2560], P(None, 'dp'), may hold values from -3 to 3
- img_size: int32 [16, 8], replicated, may hold values from 0 to 2048, as said below
- text_count: int32 [16, 8], replicated, may hold values from 0 to 128, as said below
- move_list: int32 [16, 4, 2], replicated, may hold values from 0 to 15, as said below
- w_qkv: bfloat16 [2560, 6144], P('dp', 'seq'), may hold values from -0.125 to 0.125
- qk_gain: float32 [2, 2048], P(None, 'seq'), may hold values from 0.1 to 1.9
- cotangent: bfloat16 [32768, 2048], P(('dp', 'seq')), may hold values from -6 to 6
Outputs:
- attended: bfloat16 [32768, 2048], P('dp', 'seq')
- grad_w: float32 [2560, 6144], P('dp', 'seq')
Inputs may be any that keep to these rules, and one draw needn't show every extreme that they name: `img_size`: in every group the used slots come first and tile its 2048 rows in order; every used size is 128 times a power of two, at least 256, and each image starts at a multiple of its size; unused slots are 0. `text_count`: at least 1 for a used slot, 0 for an unused one. `move_list`: in each column the 4 entries name 4 distinct groups and form one cycle: each entry's destination is the next entry's source and the last's is the first's.
All inputs are finite; a program needn't handle non-finite values.
Results may differ from a plain program's by a relative error of at most 0.014.
Values may be sent and summed in bfloat16 or wider, within the bound.
A program may use at most 128 MiB of HBM per device.

v0:
```python
import math

import jax
import jax.numpy as jnp
from jax import lax
from jax.sharding import PartitionSpec as P

EPSILON = 1e-06


def home_layout(img_size, text_count, group_rows):
    positions = jnp.arange(group_rows, dtype=jnp.int32)
    image_ends = jnp.cumsum(img_size, axis=1)
    image_index = jnp.sum(
        (positions[None, :, None] >= image_ends[:, None, :]).astype(jnp.int32), axis=2
    )
    slot_ids = jnp.arange(img_size.shape[1], dtype=jnp.int32)
    owners = (image_index[:, :, None] == slot_ids[None, None, :]).astype(jnp.int32)
    starts = jnp.sum(owners * (image_ends - img_size)[:, None, :], axis=2)
    limits = jnp.sum(owners * text_count[:, None, :], axis=2)
    is_text = positions[None, :] - starts < limits
    return (image_index, is_text)


def sources(move_list, group_count):
    group_ids = jnp.arange(group_count, dtype=jnp.int32)
    move_hits = (group_ids[:, None, None] == move_list[None, :, :, 1]).astype(jnp.int32)
    is_moved = jnp.sum(move_hits, axis=2) > 0
    anchor = jnp.sum(move_hits * move_list[None, :, :, 0], axis=2)
    return jnp.where(is_moved, anchor, group_ids[:, None])


def rms_scale(values, gain_row):
    inverse = lax.rsqrt(jnp.mean(values * values, axis=-1, keepdims=True) + EPSILON)
    return (values * inverse * gain_row, inverse)


def rms_back(values, inverse, gain_row, upstream):
    inner_mean = jnp.mean(upstream * gain_row * values, axis=-1, keepdims=True)
    return inverse * gain_row * upstream - values * (inverse * inverse * inverse) * inner_mean


def feature_term(gathered, grads):
    return lax.dot_general(
        gathered, grads, (((0,), (0,)), ((), ())), preferred_element_type=jnp.float32
    )


def body(tokens, modulation, img_size, text_count, move_list, w_qkv, qk_gain, cotangent):
    dev_rows, width = tokens.shape
    seq_count = lax.axis_size("seq")
    group_count = lax.axis_size("dp")
    group_id = lax.axis_index("dp")
    column_id = lax.axis_index("seq")
    slot_count = img_size.shape[1]
    head_size = qk_gain.shape[1]
    group_rows = seq_count * dev_rows
    score_scale = 1.0 / math.sqrt(head_size)
    full_weight = lax.all_gather(w_qkv, "dp", axis=0, tiled=True)
    image_index, is_text = home_layout(img_size, text_count, group_rows)
    own_index = lax.dynamic_slice(image_index, (group_id, column_id * dev_rows), (1, dev_rows))[0]
    own_text = lax.dynamic_slice(is_text, (group_id, column_id * dev_rows), (1, dev_rows))[0]
    selector = (own_index[:, None] == jnp.arange(slot_count, dtype=jnp.int32)[None, :]).astype(
        jnp.float32
    )
    picked = jnp.einsum("ri,cid->crd", selector, modulation, precision=lax.Precision.HIGHEST)
    token_rows = tokens.astype(jnp.float32)
    centre = jnp.mean(token_rows, axis=1, keepdims=True)
    offsets = token_rows - centre
    variance = jnp.mean(offsets * offsets, axis=1, keepdims=True)
    normed = offsets * lax.rsqrt(variance + EPSILON)
    shift_rows = jnp.where(own_text[:, None], picked[2], picked[0])
    scale_rows = jnp.where(own_text[:, None], picked[3], picked[1])
    modulated = (normed * (1.0 + scale_rows) + shift_rows).astype(jnp.bfloat16)
    anchor_all = sources(move_list, group_count)
    anchor_group = anchor_all[group_id]
    every_block = lax.all_gather(modulated, "dp", axis=0, tiled=True)
    resident = lax.dynamic_slice_in_dim(
        every_block, anchor_group[column_id] * dev_rows, dev_rows, 0
    )
    choose_group = (
        anchor_group[:, None] == jnp.arange(group_count, dtype=jnp.int32)[None, :]
    ).astype(jnp.int32)
    index_columns = image_index.reshape(group_count, seq_count, dev_rows).transpose(1, 0, 2)
    moved_index = jnp.sum(choose_group[:, :, None] * index_columns, axis=1)
    segment = (anchor_group[:, None] * slot_count + moved_index).reshape(group_rows)
    gathered = lax.all_gather(resident, "seq", axis=0, tiled=True)
    projected = jnp.dot(gathered, full_weight, preferred_element_type=jnp.float32)
    query_raw = projected[:, :head_size]
    key_raw = projected[:, head_size : 2 * head_size]
    value_raw = projected[:, 2 * head_size :]
    query_norm, query_inverse = rms_scale(query_raw, qk_gain[0])
    key_norm, key_inverse = rms_scale(key_raw, qk_gain[1])
    query_bf = query_norm.astype(jnp.bfloat16)
    key_bf = key_norm.astype(jnp.bfloat16)
    value_bf = value_raw.astype(jnp.bfloat16)
    upstream_all = lax.all_to_all(cotangent, "seq", split_axis=1, concat_axis=0, tiled=True)
    block_rows = min(512, group_rows)
    block_count = group_rows // block_rows
    blocks_in = (
        query_bf.reshape(block_count, block_rows, head_size),
        segment.reshape(block_count, block_rows),
        upstream_all.reshape(block_count, block_rows, head_size),
    )

    def attend(running, block_in):
        key_grad, value_grad = running
        query_block, segment_block, upstream = block_in
        scores = (
            lax.dot_general(
                query_block, key_bf, (((1,), (1,)), ((), ())), preferred_element_type=jnp.float32
            )
            * score_scale
        )
        same_image = segment_block[:, None] == segment[None, :]
        exponent = jnp.where(same_image, jnp.exp(scores), 0.0)
        probabilities = (exponent / jnp.sum(exponent, axis=1, keepdims=True)).astype(jnp.bfloat16)
        attended_block = jnp.dot(
            probabilities, value_bf, preferred_element_type=jnp.float32
        ).astype(jnp.bfloat16)
        row_delta = jnp.sum(
            upstream.astype(jnp.float32) * attended_block.astype(jnp.float32), axis=1, keepdims=True
        )
        value_grad = value_grad + lax.dot_general(
            probabilities, upstream, (((0,), (0,)), ((), ())), preferred_element_type=jnp.float32
        )
        value_prob_grad = lax.dot_general(
            upstream, value_bf, (((1,), (1,)), ((), ())), preferred_element_type=jnp.float32
        )
        score_grad = (
            probabilities.astype(jnp.float32) * (value_prob_grad - row_delta) * score_scale
        ).astype(jnp.bfloat16)
        query_block_grad = jnp.dot(score_grad, key_bf, preferred_element_type=jnp.float32)
        key_grad = key_grad + lax.dot_general(
            score_grad, query_block, (((0,), (0,)), ((), ())), preferred_element_type=jnp.float32
        )
        return ((key_grad, value_grad), (attended_block, query_block_grad))

    zero_grads = jnp.zeros((group_rows, head_size), jnp.float32)
    (key_norm_grad, value_grad), (attended_blocks, query_blocks) = lax.scan(
        attend, (zero_grads, zero_grads), blocks_in
    )
    attended = attended_blocks.reshape(group_rows, head_size)
    query_norm_grad = query_blocks.reshape(group_rows, head_size)
    query_grad = rms_back(query_raw, query_inverse, qk_gain[0], query_norm_grad)
    key_grad = rms_back(key_raw, key_inverse, qk_gain[1], key_norm_grad)
    head_grads = jnp.concatenate([query_grad, key_grad, value_grad], axis=1).astype(jnp.bfloat16)
    grad_w = lax.psum_scatter(
        feature_term(gathered, head_grads), "dp", scatter_dimension=0, tiled=True
    )
    return (attended, grad_w)


def solution(mesh):
    placed = (
        P(("dp", "seq"), None),
        P(None, "dp", None),
        P(),
        P(),
        P(),
        P("dp", "seq"),
        P(None, "seq"),
        P(("dp", "seq"), None),
    )
    return jax.shard_map(
        body,
        mesh=mesh,
        in_specs=placed,
        out_specs=(P("dp", "seq"), P("dp", "seq")),
        check_vma=False,
    )
```

profile of v0, /device:TPU:2, one launch (start us, length us, event | category | flops | bytes accessed | tf_op | source)
XLA Modules:
  0.0 373.3 jit_solution(4872491593257393017)
XLA Ops:
  13.6 2.2 convolution_bitcast_fusion.1
  19.3 66.8 %all-gather.4.cloned.1.call-done = bf16[2048,2560]{1,0:T(8,128)(2,1)} async-done(((bf16[128,2560]{1,0:T(8,128)(2,1)}), bf16[2048,2560]{1,0:T(8,128)(2,1)}) %all-gather.4.cloned.1.call-update) | async-done | bytes 10485776 | tf_op jit(solution)/shard_map/all_gather | solution.py:77
  89.2 7.3 %all-to-all-start = ((bf16[128,16,128]{0,2,1:T(8,128)(2,1)}), bf16[128,16,128]{0,2,1:T(8,128)(2,1)S(1)}, u32[]{:S(2)}, u32[]{:S(2)}) async-start(bf16[128,16,128]{0,2,1:T(8,128)(2,1)} %bitcast.16), calls=%async_computation | async-start | bytes 1048576 | tf_op jit(solution)/shard_map/all_to_all | solution.py:97
  97.2 9.9 %all-to-all-done = bf16[128,16,128]{0,2,1:T(8,128)(2,1)S(1)} async-done(((bf16[128,16,128]{0,2,1:T(8,128)(2,1)}), bf16[128,16,128]{0,2,1:T(8,128)(2,1)S(1)}, u32[]{:S(2)}, u32[]{:S(2)}) %all-to-all-start) | async-done | bytes 524320 | tf_op jit(solution)/shard_map/all_to_all | solution.py:97
  108.1 18.0 %all-gather.8.cloned.1.call-done = bf16[2560,384]{1,0:T(8,128)(2,1)} async-done(((bf16[160,384]{1,0:T(8,128)(2,1)}), bf16[2560,384]{1,0:T(8,128)(2,1)}) %all-gather.8.cloned.1.call-update) | async-done | bytes 1966096 | tf_op jit(solution)/shard_map/all_gather | solution.py:59
  126.0 86.6 %all-gather.6.cloned.1.call-done = bf16[2048,2560]{1,0:T(8,128)(2,1)} async-done(((bf16[128,2560]{1,0:T(8,128)(2,1)}), bf16[2048,2560]{1,0:T(8,128)(2,1)}) %all-gather.6.cloned.1.call-update) | async-done | bytes 10485776 | tf_op jit(solution)/shard_map/all_gather | solution.py:87
  212.6 8.9 %fusion.38 = f32[2048,384]{1,0:T(8,128)S(1)} fusion(bf16[2048,2560]{1,0:T(8,128)(2,1)} %all-gather.6.cloned.1.call-done, bf16[2560,384]{1,0:T(8,128)(2,1)} %all-gather.8.cloned.1.call-done), kind=kOutput, calls=%fused_computation.95 | convolution fusion | flops 4026531840 | bytes 15597568 | tf_op jit(solution)/shard_map/dot_general | solution.py:88
  223.7 63.8 %while.17 = (s32[]{:T(128)}, f32[2048,128]{1,0:T(8,128)}, f32[2048,128]{1,0:T(8,128)}, bf16[4,512,128]{2,1,0:T(8,128)(2,1)}, f32[4,512,128]{2,1,0:T(8,128)}, /*i...) while((s32[]{:T(128)}, f32[2048,128]{1,0:T(8,128)}, ...), condition=%wide.region_14.15_spmd.clone, body=%wide.region_11.14_spmd.clone.sunk | while | flops 1623522304 | bytes 48259296 | solution.py:140
  223.7 2.3 fusion.75
  230.6 3.5 convolution_add_fusion.4
  234.1 2.6 fusion.76
  239.5 2.3 fusion.75
  246.3 3.8 %convolution_add_fusion.4 = f32[2048,128]{1,0:T(8,128)} fusion(bf16[512,2048]{1,0:T(8,128)(2,1)} %multiply_convert_fusion.4, f32[2048,128]{1,0:T(8,128)} %get-tuple-element.274, pred[]{:T(512)S(6)} %compare.3, bf16[4,512,128]{2,1,0:T(8,128)(2,1)} %get-tuple-element.293, s32[]{:T(128)} %get-tuple-element.273), kind=kOutput, calls=%fused_computation.4.clone.1 | convolution fusion | flops 268959744 | bytes 4325889 | tf_op jit(solution)/shard_map/while/body/eval_jaxpr/dot_general | solution.py:134
  250.1 2.6 fusion.76
  255.5 2.3 fusion.75
  262.4 3.8 %convolution_add_fusion.4 = f32[2048,128]{1,0:T(8,128)} fusion(bf16[512,2048]{1,0:T(8,128)(2,1)} %multiply_convert_fusion.4, f32[2048,128]{1,0:T(8,128)} %get-tuple-element.274, pred[]{:T(512)S(6)} %compare.3, bf16[4,512,128]{2,1,0:T(8,128)(2,1)} %get-tuple-element.293, s32[]{:T(128)} %get-tuple-element.273), kind=kOutput, calls=%fused_computation.4.clone.1 | convolution fusion | flops 268959744 | bytes 4325889 | tf_op jit(solution)/shard_map/while/body/eval_jaxpr/dot_general | solution.py:134
  266.2 2.6 fusion.76
  271.6 2.2 fusion.75
  278.4 3.8 %convolution_add_fusion.4 = f32[2048,128]{1,0:T(8,128)} fusion(bf16[512,2048]{1,0:T(8,128)(2,1)} %multiply_convert_fusion.4, f32[2048,128]{1,0:T(8,128)} %get-tuple-element.274, pred[]{:T(512)S(6)} %compare.3, bf16[4,512,128]{2,1,0:T(8,128)(2,1)} %get-tuple-element.293, s32[]{:T(128)} %get-tuple-element.273), kind=kOutput, calls=%fused_computation.4.clone.1 | convolution fusion | flops 268959744 | bytes 4325889 | tf_op jit(solution)/shard_map/while/body/eval_jaxpr/dot_general | solution.py:134
  282.2 2.6 fusion.76
  287.6 3.0 fusion.27
  291.4 3.5 fusion.25
  294.9 9.6 %fusion.9 = f32[2560,384]{1,0:T(8,128)} fusion(bf16[2048,2560]{1,0:T(8,128)(2,1)} %all-gather.6.cloned.1.call-done, bf16[2048,128]{1,0:T(8,128)(2,1)S(1)} %convert.15, bf16[2048,128]{1,0:T(8,128)(2,1)S(1)} %get-tuple-element.172, bf16[2048,128]{1,0:T(8,128)(2,1)S(1)} %get-tuple-element.171), kind=kOutput, calls=%fused_computation.23 | convolution fusion | flops 4031250432 | bytes 15990784 | tf_op jit(solution)/shard_map/dot_general | solution.py:44
  304.5 62.2 %reduce-scatter.2.cloned.1.call-done = f32[160,384]{1,0:T(8,128)} async-done(((f32[2560,384]{1,0:T(8,128)}), f32[160,384]{1,0:T(8,128)}) %reduce-scatter.2.cloned.1.call-update) | async-done | bytes 245776 | tf_op jit(solution)/shard_map/reduce_scatter | solution.py:148
  (129 shorter events, 46.4 us)
Async XLA Ops:
  7.2 6.4 %copy-start = (f32[4,8,2560]{2,1,0:T(8,128)S(1)}, f32[4,8,2560]{2,1,0:T(8,128)}, u32[]{:S(2)}) copy-start(f32[4,8,2560]{2,1,0:T(8,128)} %param.11) | copy-start | bytes 983044
  7.2 78.9 %all-gather.4.cloned.1.call-start = ((), (), s32[]{:S(2)}) async-start(), calls=%async_computation.2 | async-start | bytes 11141120 | tf_op jit(solution)/shard_map/all_gather | solution.py:77
  13.6 2.3 copy-start.8
  15.8 2.2 copy-start.10
  17.2 70.9 %copy-start.9 = (bf16[128,2048]{1,0:T(8,128)(2,1)S(1)}, bf16[128,2048]{1,0:T(8,128)(2,1)}, u32[]{:S(2)}) copy-start(bf16[128,2048]{1,0:T(8,128)(2,1)} %param.17) | copy-start | bytes 1572868
  17.2 108.8 %all-gather.8.cloned.1.call-start = ((), (), s32[]{:S(2)}) async-start(), calls=%async_computation.4 | async-start | bytes 2088960 | tf_op jit(solution)/shard_map/all_gather | solution.py:59
  18.0 194.7 %all-gather.6.cloned.1.call-start = ((), (), s32[]{:S(2)}) async-start(), calls=%async_computation.3 | async-start | bytes 11141120 | tf_op jit(solution)/shard_map/all_gather | solution.py:87
  19.3 77.5 %copy-start.11 = (f32[2,128]{1,0:T(2,128)S(1)}, f32[2,128]{1,0:T(2,128)}, u32[]{:S(2)}) copy-start(f32[2,128]{1,0:T(2,128)} %param.16) | copy-start | bytes 3076
  89.2 17.9 %all-to-all-start = ((bf16[128,16,128]{0,2,1:T(8,128)(2,1)}), bf16[128,16,128]{0,2,1:T(8,128)(2,1)S(1)}, u32[]{:S(2)}, u32[]{:S(2)}) async-start(bf16[128,16,128]{0,2,1:T(8,128)(2,1)} %bitcast.16), calls=%async_computation | async-start | bytes 1048576 | tf_op jit(solution)/shard_map/all_to_all | solution.py:97
  96.5 270.3 %reduce-scatter.2.cloned.1.call-start = ((), (), s32[]{:S(2)}) async-start(), calls=%async_computation.5 | async-start | bytes 4177920 | tf_op jit(solution)/shard_map/reduce_scatter | solution.py:148
  221.5 2.2 copy-start.6
  230.6 3.5 copy-start.1
  234.1 2.6 copy-start.3
  237.7 1.0 copy-start.4
  246.3 3.8 %copy-start.1 = (bf16[512,2048]{1,0:T(8,128)(2,1)S(1)}, bf16[512,2048]{1,0:T(8,128)(2,1)}, u32[]{:S(2)}) copy-start(bf16[512,2048]{1,0:T(8,128)(2,1)} %multiply_convert_fusion.4) | copy-start | bytes 6291460 | tf_op jit(solution)/shard_map/while
  250.1 2.6 copy-start.3
  253.7 1.0 copy-start.4
  262.4 3.8 %copy-start.1 = (bf16[512,2048]{1,0:T(8,128)(2,1)S(1)}, bf16[512,2048]{1,0:T(8,128)(2,1)}, u32[]{:S(2)}) copy-start(bf16[512,2048]{1,0:T(8,128)(2,1)} %multiply_convert_fusion.4) | copy-start | bytes 6291460 | tf_op jit(solution)/shard_map/while
  266.1 2.6 copy-start.3
  278.4 3.8 %copy-start.1 = (bf16[512,2048]{1,0:T(8,128)(2,1)S(1)}, bf16[512,2048]{1,0:T(8,128)(2,1)}, u32[]{:S(2)}) copy-start(bf16[512,2048]{1,0:T(8,128)(2,1)} %multiply_convert_fusion.4) | copy-start | bytes 6291460 | tf_op jit(solution)/shard_map/while
  282.2 2.6 copy-start.3
  287.6 3.0 copy-start.5
  287.6 3.1 copy-start.2
  287.6 3.8 %copy-start.7 = (f32[2048,384]{1,0:T(8,128)S(1)}, f32[2048,384]{1,0:T(8,128)}, u32[]{:S(2)}) copy-start(f32[2048,384]{1,0:T(8,128)} %copy-done.6) | copy-start | bytes 9437188
  (2 other events, 2.0 us)
Sparse Core Ops, SparseCore 0:
  17.3 68.7 all-gather.3
  87.9 38.0 all-gather.7
  128.5 84.1 all-gather.5
  304.7 62.0 reduce-scatter.1
where the time goes:
time: 374 us; the launch traced here: 373 us
  waiting for transfers between devices  244 us (65%)
  matrix products  70.7 us (19%)
  other arithmetic  18 us (5%)
  local copies, waits for them, and re-layouts  17.9 us (5%)
  between operations  14.7 us (4%)
  starting transfers between devices  7.61 us (2%)
    all_gather x1, waiting for transfers between devices, body(): gathered = lax.all_gather(resident, 'seq', axis=0, tiled=True)  86.6 us
    all_gather x1, waiting for transfers between devices, body(): every_block = lax.all_gather(modulated, 'dp', axis=0, tiled=True)  66.8 us
    reduce_scatter x1, waiting for transfers between devices, body(): lax.psum_scatter(feature_term(gathered, head_grads), 'dp', scatter_dimens...  62.2 us
    all_gather x1, waiting for transfers between devices, body(): full_weight = lax.all_gather(w_qkv, 'dp', axis=0, tiled=True)  18 us
    dot_general x4, matrix products, attend(): lax.dot_general(score_grad, query_block, (((0,), (0,)), ((), ())), prefer...  14.8 us
    dot_general x4, matrix products, attend(): jnp.dot(score_grad, key_bf, preferred_element_type=jnp.float32)  10.2 us
    all_to_all x1, waiting for transfers between devices, body(): lax.all_to_all(cotangent, 'seq', split_axis=1, concat_axis=0, tiled=True)  9.88 us
    dot_general x1, matrix products, feature_term(): lax.dot_general(gathered, grads, (((0,), (0,)), ((), ())), preferred_elem...  9.64 us
  transfers between devices with their start and end apart: 5, of which 5 were waited for; matrix products, arithmetic and copies ran while one was open for 1% of the time, Pallas kernels for 0%

commit v1 on v0

v1 whole, which is shorter than its diff:
```python
import math

import jax
import jax.numpy as jnp
from jax import lax
from jax.experimental import pallas as pl
from jax.experimental.pallas import tpu as pltpu
from jax.sharding import PartitionSpec as P

EPSILON = 1e-06
MESH = pl.DeviceIdType.MESH
F32 = jnp.float32
BF16 = jnp.bfloat16
D = 2560
DH = 128
RB = 128
NC = 16
NG = 16
GR = NC * RB
CHUNKS = 5
CW = D // CHUNKS
PW = CW // 2
HALF = RB // 2
QUART = HALF // 2
SHARD = D // NG
TN = (((0,), (0,)), ((), ()))
NT = (((1,), (1,)), ((), ()))
VMEM_LIMIT = 60 << 20


def aligned(value, step):
    return pl.multiple_of(value, step)


def anchor_of(mv, column, group):
    anchor = group
    for k in range(4):
        anchor = jnp.where(mv[column, 2 * k + 1] == group, mv[column, 2 * k], anchor)
    return anchor


def gather_kernel(
    img, txt, mv, tok, mod, w, cot,
    gout, proj, up,
    modv, sa, sb, sc, sd, se, st2, gath, wfull,
    m1s, m1r, m2s, m2r, gs, gr, wus, wur, wds, wdr, wss, wsr, wl, cs, cr, ls,
):
    dp = lax.axis_index("dp")
    sq = lax.axis_index("seq")
    z, core = dp // 2, dp % 2
    y, x = sq // 4, sq % 4
    st1 = (sa, sb, sc, sd, se)

    barrier = pltpu.get_barrier_semaphore()

    @pl.loop(1, 16)
    def _(k):
        pl.semaphore_signal(
            barrier, inc=1, device_id={"dp": lax.rem(dp + k, 16)}, device_id_type=MESH
        )
        pl.semaphore_signal(
            barrier, inc=1, device_id={"seq": lax.rem(sq + k, 16)}, device_id_type=MESH
        )

    first = sq * RB
    slot = jnp.int32(0)
    start = jnp.int32(0)
    end = jnp.int32(0)
    for i in range(8):
        end = end + img[dp, i]
        hit = first >= end
        slot = slot + hit.astype(jnp.int32)
        start = jnp.where(hit, end, start)
    slot = jnp.minimum(slot, 7)
    limit = txt[dp, slot] - (first - start)

    @pl.loop(0, RB // 16)
    def _(i):
        r0 = aligned(i * 16, 16)
        rows = tok[pl.ds(r0, 16), :].astype(F32)
        centre = jnp.mean(rows, axis=1, keepdims=True)
        offsets = rows - centre
        variance = jnp.mean(offsets * offsets, axis=1, keepdims=True)
        normed = offsets * lax.rsqrt(variance + EPSILON)
        is_text = lax.broadcasted_iota(jnp.int32, (16, 1), 0) + r0 < limit
        shift = jnp.where(is_text, mod[2, pl.ds(slot, 1), :], mod[0, pl.ds(slot, 1), :])
        scale = jnp.where(is_text, mod[3, pl.ds(slot, 1), :], mod[1, pl.ds(slot, 1), :])
        modv[pl.ds(r0, 16), :] = (normed * (1.0 + scale) + shift).astype(BF16)

    pl.semaphore_wait(barrier, 30)

    def cot_copy(h):
        return pltpu.make_async_remote_copy(
            cot.at[:, pl.ds(aligned(h * DH, DH), DH)],
            up.at[pl.ds(aligned(sq * RB, RB), RB), :],
            cs, cr, device_id={"seq": h}, device_id_type=MESH,
        )

    def send_cot():
        pltpu.make_async_copy(
            cot.at[:, pl.ds(aligned(sq * DH, DH), DH)],
            up.at[pl.ds(aligned(sq * RB, RB), RB), :],
            cr,
        ).start()

        @pl.loop(1, 16)
        def _(k):
            cot_copy(lax.rem(sq + k, 16)).start()

    def send_m1(t):
        def piece(d):
            return modv.at[
                pl.ds(aligned(d // 2 * 16, 16), 16),
                pl.ds(aligned(t * CW + d % 2 * PW, PW), PW),
            ]

        pltpu.make_async_copy(piece(dp), st1[t].at[dp], m1r.at[t]).start()

        @pl.loop(1, 16)
        def _(k):
            d = lax.rem(dp + k, 16)
            pltpu.make_async_remote_copy(
                piece(d), st1[t].at[dp], m1s.at[t], m1r.at[t],
                device_id={"dp": d}, device_id_type=MESH,
            ).start()

    def send_m2(t):
        pltpu.make_async_copy(st1[t], st1[t], m1r.at[t]).wait()

        @pl.loop(0, 16)
        def _(d):
            st2[t, d] = st1[t][anchor_of(mv, sq, d)]

        place = gath.at[
            pl.ds(aligned(sq * RB + dp // 2 * 16, 16), 16),
            pl.ds(aligned(t * CW + dp % 2 * PW, PW), PW),
        ]
        pltpu.make_async_copy(st2.at[t, dp], place, m2r.at[t]).start()

        @pl.loop(1, 16)
        def _(k):
            d = lax.rem(dp + k, 16)
            pltpu.make_async_remote_copy(
                st2.at[t, d], place, m2s.at[t], m2r.at[t],
                device_id={"dp": d}, device_id_type=MESH,
            ).start()

    def column(h, i, j):
        if h == 0:
            return lax.rem(y + j + 4, 4) * 4 + lax.rem(x + i + 4, 4)
        return lax.rem(y + i + 4, 4) * 4 + lax.rem(x + j + 4, 4)

    def beside(along_x, step):
        if along_x:
            return {"seq": y * 4 + lax.rem(x + step + 4, 4)}
        return {"seq": lax.rem(y + step + 4, 4) * 4 + x}

    def region(t, h, i, j, part):
        low = column(h, i, j) * RB + h * HALF + (QUART if part == 2 else 0)
        count = HALF if part == 0 else QUART
        return gath.at[pl.ds(aligned(low, QUART), count), pl.ds(t * CW, CW)]

    offsets = (0, -1, 1, 2)

    def event(t, h, e):
        if e < 4:
            along_x = h == 0
            i, j = {0: (0, 0), 1: (0, 0), 2: (-1, 0), 3: (1, 0)}[e]
            gi, gj = {0: (-1, 0), 1: (1, 0), 2: (2, 0), 3: (2, 0)}[e]
            kind = e
        else:
            along_x = h == 1
            k, kind = (e - 4) // 4, (e - 4) % 4
            o = offsets[k]
            i, j = o, {0: 0, 1: 0, 2: -1, 3: 1}[kind]
            gi, gj = o, {0: -1, 1: 1, 2: 2, 3: 2}[kind]
        part = {0: 0, 1: 0, 2: 1, 3: 2}[kind]
        step = 1 if kind in (0, 2) else -1
        return (i, j, gi, gj, part, along_x, step)

    def put(t, h, e):
        i, j, _, _, part, along_x, step = event(t, h, e)
        place = region(t, h, i, j, part)
        pltpu.make_async_remote_copy(
            place, place, gs.at[t, h, e], gr.at[t, h, e],
            device_id=beside(along_x, step), device_id_type=MESH,
        ).start()

    def got(t, h, e):
        _, _, gi, gj, part, _, _ = event(t, h, e)
        place = region(t, h, gi, gj, part)
        pltpu.make_async_copy(place, place, gr.at[t, h, e]).wait()

    def sent(t, h, e):
        i, j, _, _, part, _, _ = event(t, h, e)
        place = region(t, h, i, j, part)
        pltpu.make_async_copy(place, place, gs.at[t, h, e]).wait()

    def stage2(t):
        place = gath.at[pl.ds(aligned(sq * RB, RB), RB), pl.ds(t * CW, CW)]
        pltpu.make_async_copy(place, place, m2r.at[t]).wait()
        for e in (0, 1, 4, 5):
            for h in (0, 1):
                put(t, h, e)

    def stage3(t):
        for h in (0, 1):
            got(t, h, 0)
            for e in (2, 8, 9):
                put(t, h, e)
        for h in (0, 1):
            got(t, h, 1)
            for e in (3, 12, 13):
                put(t, h, e)
        for h in (0, 1):
            for kind in (0, 1):
                got(t, h, 4 + kind)
                put(t, h, 6 + kind)

    def stage4(t):
        for h in (0, 1):
            got(t, h, 2)
            got(t, h, 3)
            for e in (16, 17):
                put(t, h, e)
        for k in (1, 2):
            for h in (0, 1):
                for kind in (0, 1):
                    got(t, h, 4 + 4 * k + kind)
                    put(t, h, 6 + 4 * k + kind)

    def stage5(t):
        for h in (0, 1):
            for kind in (0, 1):
                got(t, h, 16 + kind)
                put(t, h, 18 + kind)

    def stage6(t):
        for h in (0, 1):
            for k in range(4):
                got(t, h, 6 + 4 * k)
                got(t, h, 7 + 4 * k)
        pltpu.make_async_copy(
            gath.at[:, pl.ds(t * CW, CW)], gout.at[:, pl.ds(t * CW, CW)], ls.at[t]
        ).start()

        @pl.loop(0, GR // 256)
        def _(i):
            r0 = aligned(i * 256, 256)
            term = jnp.dot(
                gath[pl.ds(r0, 256), pl.ds(t * CW, CW)],
                wfull[pl.ds(t * CW, CW), :],
                preferred_element_type=F32,
            )
            if t == 0:
                proj[pl.ds(r0, 256), :] = term
            else:
                proj[pl.ds(r0, 256), :] += term

    def shard(dz, c):
        return wfull.at[pl.ds(aligned((lax.rem(z + dz + 8, 8) * 2 + c) * SHARD, 16), SHARD), :]

    def to_z(step):
        return {"dp": lax.rem(z + step + 8, 8) * 2 + core}

    def w_put(src, dst, ssem, rsem, device):
        pltpu.make_async_remote_copy(
            src, dst, ssem, rsem, device_id=device, device_id_type=MESH
        ).start()

    def w_got(place, sem):
        pltpu.make_async_copy(place, place, sem).wait()

    other = {"dp": z * 2 + 1 - core}

    def weights(step):
        if step == 0:
            own = shard(0, core)
            pltpu.make_async_copy(w, own, wl).start()
            w_put(w, own, wus.at[0], wur.at[0], to_z(1))
            w_put(w, own, wds.at[0], wdr.at[0], to_z(-1))
            w_put(w, own, wss.at[0], wsr.at[0], other)
            return
        if step <= 4:
            place = shard(-step, core)
            w_got(place, wur.at[step - 1])
            if step < 4:
                w_put(place, place, wus.at[step], wur.at[step], to_z(1))
            w_put(place, place, wss.at[step], wsr.at[step], other)
        if step <= 3:
            place = shard(step, core)
            w_got(place, wdr.at[step - 1])
            if step < 3:
                w_put(place, place, wds.at[step], wdr.at[step], to_z(-1))
            w_put(place, place, wss.at[4 + step], wsr.at[4 + step], other)

    sib_order = (0, -1, -2, -3, -4, 1, 2, 3)

    def weights_end():
        w_got(shard(0, core), wl)
        for k in range(8):
            w_got(shard(sib_order[k], 1 - core), wsr.at[k])

    send_m1(0)
    send_cot()
    send_m1(1)
    stages = ((5, stage5), (4, stage4), (3, stage3), (2, stage2))
    for n in range(CHUNKS + 5):
        for s, run in stages:
            t = n - s + 1
            if 0 <= t < CHUNKS:
                run(t)
        if n < CHUNKS:
            send_m2(n)
        if n + 2 < CHUNKS:
            send_m1(n + 2)
        if n <= 4:
            weights(n)
        if n == 5:
            weights_end()
        t = n - 5
        if 0 <= t < CHUNKS:
            stage6(t)

    pltpu.make_async_copy(up, up, cr).wait()
    part = up.at[pl.ds(0, 15 * RB), :]
    pltpu.make_async_copy(part, part, cs).wait()
    for t in range(CHUNKS):
        part = st1[t].at[pl.ds(0, 15)]
        pltpu.make_async_copy(part, part, m1s.at[t]).wait()
        pltpu.make_async_copy(part, part, m2s.at[t]).wait()
        for h in (0, 1):
            for e in range(20):
                sent(t, h, e)
        pltpu.make_async_copy(
            gath.at[:, pl.ds(t * CW, CW)], gout.at[:, pl.ds(t * CW, CW)], ls.at[t]
        ).wait()
    own = shard(0, core)
    for k in range(4):
        w_got(own, wus.at[k])
    for k in range(3):
        w_got(own, wds.at[k])
    for k in range(8):
        w_got(own, wss.at[k])


def gather_call(img, txt, mv, tok, mod, w, cot):
    vmem = pl.BlockSpec(memory_space=pltpu.VMEM)
    smem = pl.BlockSpec(memory_space=pltpu.SMEM)
    hbm = pl.BlockSpec(memory_space=pl.ANY)
    dma = pltpu.SemaphoreType.DMA
    return pl.pallas_call(
        gather_kernel,
        name="gather_project",
        out_shape=(
            jax.ShapeDtypeStruct((GR, D), BF16),
            jax.ShapeDtypeStruct((GR, 3 * DH), F32),
            jax.ShapeDtypeStruct((GR, DH), BF16),
        ),
        in_specs=[smem, smem, smem, vmem, vmem, hbm, hbm],
        out_specs=(hbm, vmem, hbm),
        scratch_shapes=[
            pltpu.VMEM((RB, D), BF16),
            *[pltpu.VMEM((16, 16, PW), BF16)] * CHUNKS,
            pltpu.VMEM((CHUNKS, 16, 16, PW), BF16),
            pltpu.VMEM((GR, D), BF16),
            pltpu.VMEM((D, 3 * DH), BF16),
            dma((CHUNKS,)), dma((CHUNKS,)), dma((CHUNKS,)), dma((CHUNKS,)),
            dma((CHUNKS, 2, 20)), dma((CHUNKS, 2, 20)),
            dma((4,)), dma((4,)), dma((3,)), dma((3,)), dma((8,)), dma((8,)), dma(()),
            dma(()), dma(()), dma((CHUNKS,)),
        ],
        compiler_params=pltpu.CompilerParams(
            collective_id=0, has_side_effects=True, vmem_limit_bytes=VMEM_LIMIT
        ),
    )(img, txt, mv, tok, mod, w, cot)


MASK = 4096.0


def attention_kernel(
    img, mv, proj, up, gain,
    att, hg,
    qx, kx, vx, ux, us, es, dq, dk, dv, place, back, low, high,
):
    group = lax.axis_index("dp")
    scale = 1.0 / math.sqrt(DH)
    segs = []
    for c in range(NC):
        anchor = anchor_of(mv, c, group)
        slot = jnp.int32(0)
        end = jnp.int32(0)
        for i in range(8):
            end = end + img[anchor, i]
            slot = slot + (c * RB >= end).astype(jnp.int32)
        segs.append(anchor * 8 + slot)
    for c in range(NC):
        less = jnp.int32(0)
        same = jnp.int32(0)
        ahead = jnp.int32(0)
        for o in range(NC):
            less = less + (segs[o] < segs[c]).astype(jnp.int32)
            equal = (segs[o] == segs[c]).astype(jnp.int32)
            same = same + equal
            if o < c:
                ahead = ahead + equal
        spot = less + ahead
        place[c] = spot
        back[spot] = c
        low[spot] = less
        high[spot] = less + same

    lanes = lax.broadcasted_iota(jnp.int32, (RB, DH), 1)
    gain_q = gain[0:1, :]
    gain_k = gain[1:2, :]

    @pl.loop(0, NC)
    def _(c):
        r0 = aligned(c * RB, RB)
        spot = place[c]
        s0 = aligned(spot * RB, RB)
        mark = low[spot]
        q = proj[pl.ds(r0, RB), 0:DH]
        k = proj[pl.ds(r0, RB), DH : 2 * DH]
        qi = lax.rsqrt(jnp.mean(q * q, axis=1, keepdims=True) + EPSILON)
        ki = lax.rsqrt(jnp.mean(k * k, axis=1, keepdims=True) + EPSILON)
        qx[pl.ds(s0, RB), 0:DH] = (q * qi * gain_q).astype(BF16)
        kx[pl.ds(s0, RB), 0:DH] = (k * ki * gain_k).astype(BF16)
        vx[pl.ds(s0, RB), 0:DH] = proj[pl.ds(r0, RB), 2 * DH : 3 * DH].astype(BF16)
        hot = lanes == mark
        tail = lanes == NC
        qx[pl.ds(s0, RB), DH:] = jnp.where(hot, MASK, jnp.where(tail, 1.0, 0.0)).astype(BF16)
        kx[pl.ds(s0, RB), DH:] = jnp.where(hot, 1.0, jnp.where(tail, -MASK, 0.0)).astype(BF16)
        vx[pl.ds(s0, RB), DH:] = jnp.where(lanes < 2, -1.0, 0.0).astype(BF16)
        us[pl.ds(s0, RB), :] = up[pl.ds(r0, RB), :]

    dk[...] = jnp.zeros_like(dk)
    dv[...] = jnp.zeros_like(dv)
    wide = lax.broadcasted_iota(jnp.int32, (2 * RB, DH), 1)
    factor = scale * math.log2(math.e)

    @pl.loop(0, NC // 2)
    def _(qt):
        q0 = aligned(qt * 2 * RB, 2 * RB)
        first = low[2 * qt] // 2
        last = (high[2 * qt + 1] + 1) // 2
        q_tile = qx[pl.ds(q0, 2 * RB), :]

        def forward(kt, total):
            k0 = aligned(kt * 2 * RB, 2 * RB)
            scores = lax.dot_general(
                q_tile, kx[pl.ds(k0, 2 * RB), :], NT, preferred_element_type=F32
            )
            e = jnp.exp2(scores * factor).astype(BF16)
            es[kt] = e
            return total + jnp.dot(e, vx[pl.ds(k0, 2 * RB), :], preferred_element_type=F32)

        total = lax.fori_loop(first, last, forward, jnp.zeros((2 * RB, 2 * DH), F32))
        inverse = -1.0 / total[:, DH : DH + 1]
        out = (total[:, :DH] * inverse).astype(BF16)
        for b in range(2):
            att[pl.ds(aligned(back[2 * qt + b] * RB, RB), RB), :] = out[b * RB : (b + 1) * RB]
        u = us[pl.ds(q0, 2 * RB), :].astype(F32)
        delta = jnp.sum(u * out.astype(F32), axis=1, keepdims=True) * inverse
        coarse = delta.astype(BF16).astype(F32)
        fine = delta - coarse
        u_tile = (u * inverse).astype(BF16)
        ux[:, :DH] = u_tile
        ux[:, DH:] = jnp.where(wide == 0, coarse, jnp.where(wide == 1, fine, 0.0)).astype(BF16)

        def backward(kt, grad):
            k0 = aligned(kt * 2 * RB, 2 * RB)
            e = es[kt]
            inner = lax.dot_general(
                ux[...], vx[pl.ds(k0, 2 * RB), :], NT, preferred_element_type=F32
            )
            ds = (e.astype(F32) * inner).astype(BF16)
            dv[pl.ds(k0, 2 * RB), :] += lax.dot_general(
                e, ux[:, :DH], TN, preferred_element_type=F32
            )
            dk[pl.ds(k0, 2 * RB), :] += lax.dot_general(
                ds, qx[pl.ds(q0, 2 * RB), :DH], TN, preferred_element_type=F32
            )
            return grad + jnp.dot(ds, kx[pl.ds(k0, 2 * RB), :DH], preferred_element_type=F32)

        dq[pl.ds(q0, 2 * RB), :] = lax.fori_loop(
            first, last, backward, jnp.zeros((2 * RB, DH), F32)
        )

    @pl.loop(0, NC)
    def _(c):
        r0 = aligned(c * RB, RB)
        s0 = aligned(place[c] * RB, RB)

        def back_norm(values, gains, upstream):
            inverse = lax.rsqrt(jnp.mean(values * values, axis=1, keepdims=True) + EPSILON)
            scaled = upstream * gains
            inner = jnp.mean(scaled * values, axis=1, keepdims=True)
            return inverse * scaled - values * (inverse * inverse * inverse * inner)

        q = proj[pl.ds(r0, RB), 0:DH]
        k = proj[pl.ds(r0, RB), DH : 2 * DH]
        hg[pl.ds(r0, RB), 0:DH] = back_norm(q, gain_q, dq[pl.ds(s0, RB), :] * scale).astype(BF16)
        hg[pl.ds(r0, RB), DH : 2 * DH] = back_norm(
            k, gain_k, dk[pl.ds(s0, RB), :] * scale
        ).astype(BF16)
        hg[pl.ds(r0, RB), 2 * DH :] = dv[pl.ds(s0, RB), :].astype(BF16)


def attention_call(img, mv, proj, up, gain):
    vmem = pl.BlockSpec(memory_space=pltpu.VMEM)
    smem = pl.BlockSpec(memory_space=pltpu.SMEM)
    return pl.pallas_call(
        attention_kernel,
        name="attention",
        out_shape=(
            jax.ShapeDtypeStruct((GR, DH), BF16),
            jax.ShapeDtypeStruct((GR, 3 * DH), BF16),
        ),
        in_specs=[smem, smem, vmem, vmem, vmem],
        out_specs=(vmem, vmem),
        scratch_shapes=[
            pltpu.VMEM((GR, 2 * DH), BF16),
            pltpu.VMEM((GR, 2 * DH), BF16),
            pltpu.VMEM((GR, 2 * DH), BF16),
            pltpu.VMEM((2 * RB, 2 * DH), BF16),
            pltpu.VMEM((GR, DH), BF16),
            pltpu.VMEM((NC // 2, 2 * RB, 2 * RB), BF16),
            pltpu.VMEM((GR, DH), F32),
            pltpu.VMEM((GR, DH), F32),
            pltpu.VMEM((GR, DH), F32),
            pltpu.SMEM((NC,), jnp.int32),
            pltpu.SMEM((NC,), jnp.int32),
            pltpu.SMEM((NC,), jnp.int32),
            pltpu.SMEM((NC,), jnp.int32),
        ],
        compiler_params=pltpu.CompilerParams(vmem_limit_bytes=VMEM_LIMIT),
    )(img, mv, proj, up, gain)


STEPS = (2, 3, 1, 0)
FC = 4 * SHARD


def reduce_kernel(
    rows, hg, grad,
    xs, dw, pair, su, ru, sd, rd,
    xsem, ps, pr, us, ur, ds, dr,
):
    dp = lax.axis_index("dp")
    z, core = dp // 2, dp % 2
    other = {"dp": z * 2 + 1 - core}

    def to_z(step):
        return {"dp": lax.rem(z + step + 8, 8) * 2 + core}

    def chunk(n):
        return lax.rem(z // 2 + STEPS[n], 4)

    def load(n):
        return pltpu.make_async_copy(
            rows.at[:, pl.ds(aligned(chunk(n) * FC, 128), FC)], xs.at[n], xsem.at[n]
        )

    for n in range(4):
        load(n).start()
    barrier = pltpu.get_barrier_semaphore()
    for device in (other, to_z(1), to_z(-1)):
        pl.semaphore_signal(barrier, inc=1, device_id=device, device_id_type=MESH)

    def compute(n):
        load(n).wait()
        m = chunk(n)
        dw[m] = lax.dot_general(xs[n], hg[...], TN, preferred_element_type=F32)

    def pair_copy(n, j):
        m = chunk(n)
        return pltpu.make_async_remote_copy(
            dw.at[m, pl.ds(aligned((2 * j + 1 - core) * SHARD, 16), SHARD), :],
            pair.at[2 * m + j],
            ps.at[n, j], pr.at[n, j], device_id=other, device_id_type=MESH,
        )

    def pair_send(n):
        for j in range(2):
            pair_copy(n, j).start()

    def pair_wait(n):
        for j in range(2):
            pair_copy(n, j).wait_recv()

    def part(dz):
        zz = lax.rem(z + dz + 8, 8)
        at = aligned((lax.rem(zz, 2) * 2 + core) * SHARD, 16)
        return dw[zz // 2, pl.ds(at, SHARD), :] + pair[zz]

    def up_copy(k):
        return pltpu.make_async_remote_copy(
            su.at[k], ru.at[k], us.at[k], ur.at[k], device_id=to_z(1), device_id_type=MESH
        )

    def down_copy(k):
        return pltpu.make_async_remote_copy(
            sd.at[k], rd.at[k], ds.at[k], dr.at[k], device_id=to_z(-1), device_id_type=MESH
        )

    def go_up(k):
        value = part(4 - k)
        if k:
            up_copy(k - 1).wait_recv()
            value = value + ru[k - 1].astype(F32)
        su[k] = value.astype(BF16)
        up_copy(k).start()

    def go_down(k):
        value = part(k - 3)
        if k:
            down_copy(k - 1).wait_recv()
            value = value + rd[k - 1].astype(F32)
        sd[k] = value.astype(BF16)
        down_copy(k).start()

    compute(0)
    pl.semaphore_wait(barrier, 3)
    pair_send(0)
    compute(1)
    pair_send(1)
    pair_wait(0)
    go_up(0)
    compute(2)
    pair_send(2)
    pair_wait(1)
    go_down(0)
    compute(3)
    pair_send(3)
    pair_wait(2)
    go_up(1)
    go_down(1)
    go_up(2)
    pair_wait(3)
    go_down(2)
    go_up(3)
    total = part(0)
    down_copy(2).wait_recv()
    total = total + rd[2].astype(F32)
    up_copy(3).wait_recv()
    grad[...] = total + ru[3].astype(F32)
    for n in range(4):
        for j in range(2):
            pair_copy(n, j).wait_send()
    for k in range(4):
        up_copy(k).wait_send()
    for k in range(3):
        down_copy(k).wait_send()


def reduce_call(rows, hg):
    vmem = pl.BlockSpec(memory_space=pltpu.VMEM)
    hbm = pl.BlockSpec(memory_space=pl.ANY)
    dma = pltpu.SemaphoreType.DMA
    wide = 3 * DH
    return pl.pallas_call(
        reduce_kernel,
        name="grad_reduce",
        out_shape=jax.ShapeDtypeStruct((SHARD, wide), F32),
        in_specs=[hbm, vmem],
        out_specs=vmem,
        scratch_shapes=[
            pltpu.VMEM((4, GR, FC), BF16),
            pltpu.VMEM((4, FC, wide), F32),
            pltpu.VMEM((8, SHARD, wide), F32),
            pltpu.VMEM((4, SHARD, wide), BF16),
            pltpu.VMEM((4, SHARD, wide), BF16),
            pltpu.VMEM((3, SHARD, wide), BF16),
            pltpu.VMEM((3, SHARD, wide), BF16),
            dma((4,)), dma((4, 2)), dma((4, 2)), dma((4,)), dma((4,)), dma((3,)), dma((3,)),
        ],
        compiler_params=pltpu.CompilerParams(
            collective_id=1, has_side_effects=True, vmem_limit_bytes=VMEM_LIMIT
        ),
    )(rows, hg)


def body(tokens, modulation, img_size, text_count, move_list, w_qkv, qk_gain, cotangent):
    moves = move_list.reshape(NC, 8)
    gathered, projected, upstream = gather_call(
        img_size, text_count, moves, tokens, modulation, w_qkv, cotangent
    )
    attended, head_grads = attention_call(img_size, moves, projected, upstream, qk_gain)
    return (attended, reduce_call(gathered, head_grads))


def solution(mesh):
    placed = (
        P(("dp", "seq"), None),
        P(None, "dp", None),
        P(),
        P(),
        P(),
        P("dp", "seq"),
        P(None, "seq"),
        P(("dp", "seq"), None),
    )
    return jax.shard_map(
        body,
        mesh=mesh,
        in_specs=placed,
        out_specs=(P("dp", "seq"), P("dp", "seq")),
        check_vma=False,
    )
```

time: 374 us -> 179 us (0.48)
  waiting for transfers between devices: 244 us -> 0 us
  Pallas kernels: 0 us -> 171 us
  matrix products: 70.7 us -> 0 us
  other arithmetic: 18 us -> 0 us
  between operations: 14.7 us -> 0.65 us
  local copies, waits for them, and re-layouts: 17.9 us -> 5.71 us
  starting transfers between devices: 7.61 us -> 0 us
    pallas_call x0 -> x3, Pallas kernels: none -> 171 us  [the longest x1 91.7 us: gather_call(): pl.pallas_call(gather_kernel, name='gather_project', out_shape=(jax.Shape...]
    all_gather x3 -> x0, waiting for transfers between devices: 171 us -> none  [the longest x1 86.6 us: body(): gathered = lax.all_gather(resident, 'seq', axis=0, tiled=True)]
    dot_general x27 -> x0, matrix products: 70.7 us -> none  [the longest x4 14.8 us: attend(): lax.dot_general(score_grad, query_block, (((0,), (0,)), ((), ())), prefer...]
    reduce_scatter x1 -> x0, waiting for transfers between devices: 62.2 us -> none  [body(): lax.psum_scatter(feature_term(gathered, head_grads), 'dp', scatter_dimens...]
    all_to_all x1 -> x0, waiting for transfers between devices: 9.88 us -> none  [body(): lax.all_to_all(cotangent, 'seq', split_axis=1, concat_axis=0, tiled=True)]
    reduce_sum x8 -> x0, other arithmetic: 7.48 us -> none  [the longest x1 2.97 us: rms_back(): inner_mean = jnp.mean(upstream * gain_row * values, axis=-1, keepdims=True)]
    all_to_all x1 -> x0, starting transfers between devices: 7.27 us -> none  [body(): lax.all_to_all(cotangent, 'seq', split_axis=1, concat_axis=0, tiled=True)]
    dynamic_slice x14 -> x0, local copies, waits for them, and re-layouts: 6.74 us -> none  [the longest x12 4.16 us: body(): lax.scan(attend, (zero_grads, zero_grads), blocks_in)]
  transfers between devices with their start and end apart: 5 -> 0, of which waited for: 5 -> 0; matrix products, arithmetic and copies ran while one was open for 1% -> 0% of each run, Pallas kernels for 0% -> 0%
where the time goes in v1:
time: 179 us; the launch traced here: 178 us
  Pallas kernels  171 us (96%)
  local copies, waits for them, and re-layouts  5.71 us (3%)
    pallas_call x1, Pallas kernels, gather_call(): pl.pallas_call(gather_kernel, name='gather_project', out_shape=(jax.Shape...  91.7 us
    pallas_call x1, Pallas kernels, reduce_call(): pl.pallas_call(reduce_kernel, name='grad_reduce', out_shape=jax.ShapeDtyp...  57.8 us
    pallas_call x1, Pallas kernels, attention_call(): pl.pallas_call(attention_kernel, name='attention', out_shape=(jax.ShapeDt...  21.9 us
    unnamed x3, local copies, waits for them, and re-layouts  4.36 us

profile of v1, /device:TPU:2, one launch (start us, length us, event | category | flops | bytes accessed | tf_op | source)
XLA Modules:
  0.0 177.8 jit_solution(5547119243335178720)
XLA Ops:
  0.6 1.4 copy.13.img
  2.0 1.3 copy.14.mv
  3.3 1.4 copy.11.txt
  4.7 91.7 %gather_project.1 = (bf16[2048,2560]{1,0:T(8,128)(2,1)}, f32[2048,384]{1,0:T(8,128)}, bf16[2048,128]{1,0:T(8,128)(2,1)}) custom-call(s32[16,8]{1,0:T(8,128)} %copy.13.img, s32[16,8]{1,0:T(8,128)} %copy.11.txt, s32[16,8]{1,0:T(8,128)} %copy.14.mv, bf16[128,2560]{1,0:T(8,128)(2,1)} %tok.1, f32[4,8,2560]{2,1,0:T(8,128)} %mod.1, bf16[160,384]{1,0:T(8,128)(2,1)} %w.1, ...), custom_call_target="tpu_custom_call" | custom-call | tf_op jit(solution)/shard_map/gather_project/pallas_call | solution.py:352
  96.4 21.9 %attention.1 = (bf16[2048,128]{1,0:T(8,128)(2,1)}, bf16[2048,384]{1,0:T(8,128)(2,1)}) custom-call(s32[16,8]{1,0:T(8,128)} %copy.13.img, s32[16,8]{1,0:T(8,128)} %copy.14.mv, f32[2048,384]{1,0:T(8,128)} %get-tuple-element.7.proj, bf16[2048,128]{1,0:T(8,128)(2,1)} %get-tuple-element.8.up, f32[2,128]{1,0:T(2,128)} %gain.1), custom_call_target="tpu_custom_call" | custom-call | tf_op jit(solution)/shard_map/attention/pallas_call | solution.py:514
  118.3 57.8 %grad_reduce.1 = f32[160,384]{1,0:T(8,128)} custom-call(bf16[2048,2560]{1,0:T(8,128)(2,1)} %get-tuple-element.10.rows, bf16[2048,384]{1,0:T(8,128)(2,1)} %get-tuple-element.11.hg), custom_call_target="tpu_custom_call" | custom-call | tf_op jit(solution)/shard_map/grad_reduce/pallas_call | solution.py:663
  176.2 1.7 copy.16

commit v2 on v1

--- a/solution.py
+++ b/solution.py
@@ -23,6 +23,7 @@
 HALF = RB // 2
 QUART = HALF // 2
 SHARD = D // NG
+LAST = (6, 7, 10, 11, 14, 15, 18, 19)
 TN = (((0,), (0,)), ((), ()))
 NT = (((1,), (1,)), ((), ()))
 VMEM_LIMIT = 60 << 20
@@ -35,44 +36,52 @@
 def anchor_of(mv, column, group):
     anchor = group
     for k in range(4):
-        anchor = jnp.where(mv[column, 2 * k + 1] == group, mv[column, 2 * k], anchor)
+        anchor = jnp.where(mv[k, 1, column] == group, mv[k, 0, column], anchor)
     return anchor
 
 
 def gather_kernel(
     img, txt, mv, tok, mod, w, cot,
     gout, proj, up,
-    modv, sa, sb, sc, sd, se, st2, gath, wfull,
-    m1s, m1r, m2s, m2r, gs, gr, wus, wur, wds, wdr, wss, wsr, wl, cs, cr, ls,
+    modv, *scratch,
 ):
+    st1 = scratch[:CHUNKS]
+    st2, gath, wfull, m1s, m1r, m2s, m2r, gs, gr, gf, *scratch = scratch[CHUNKS:]
+    wus, wur, wds, wdr, wss, wsr, wl, cs, cr, ls = scratch
     dp = lax.axis_index("dp")
     sq = lax.axis_index("seq")
     z, core = dp // 2, dp % 2
     y, x = sq // 4, sq % 4
-    st1 = (sa, sb, sc, sd, se)
 
     barrier = pltpu.get_barrier_semaphore()
 
-    @pl.loop(1, 16)
-    def _(k):
+    groups = [lax.rem(dp + k, 16) for k in range(16)]
+    columns = [lax.rem(sq + k, 16) for k in range(16)]
+    for k in range(1, 16):
         pl.semaphore_signal(
-            barrier, inc=1, device_id={"dp": lax.rem(dp + k, 16)}, device_id_type=MESH
+            barrier, inc=1, device_id={"dp": groups[k]}, device_id_type=MESH
         )
         pl.semaphore_signal(
-            barrier, inc=1, device_id={"seq": lax.rem(sq + k, 16)}, device_id_type=MESH
-        )
+            barrier, inc=1, device_id={"seq": columns[k]}, device_id_type=MESH
+        )
+    piece_rows = [aligned(d // 2 * 16, 16) for d in groups]
+    piece_cols = [aligned(lax.rem(d, 2) * PW, PW) for d in groups]
+    ys = [lax.rem(y + k, 4) for k in range(4)]
+    xs = [lax.rem(x + k, 4) for k in range(4)]
+    bases = [[(ys[j] * 4 + xs[i]) * RB for i in range(4)] for j in range(4)]
+    anchors = [anchor_of(mv, sq, d) for d in range(16)]
 
     first = sq * RB
     slot = jnp.int32(0)
     start = jnp.int32(0)
     end = jnp.int32(0)
     for i in range(8):
-        end = end + img[dp, i]
+        end = end + img[i, dp]
         hit = first >= end
         slot = slot + hit.astype(jnp.int32)
         start = jnp.where(hit, end, start)
     slot = jnp.minimum(slot, 7)
-    limit = txt[dp, slot] - (first - start)
+    limit = txt[slot, dp] - (first - start)
 
     @pl.loop(0, RB // 16)
     def _(i):
@@ -103,60 +112,46 @@
             cr,
         ).start()
 
-        @pl.loop(1, 16)
-        def _(k):
-            cot_copy(lax.rem(sq + k, 16)).start()
+        for k in range(1, 16):
+            cot_copy(columns[k]).start()
 
     def send_m1(t):
-        def piece(d):
-            return modv.at[
-                pl.ds(aligned(d // 2 * 16, 16), 16),
-                pl.ds(aligned(t * CW + d % 2 * PW, PW), PW),
-            ]
-
-        pltpu.make_async_copy(piece(dp), st1[t].at[dp], m1r.at[t]).start()
-
-        @pl.loop(1, 16)
-        def _(k):
-            d = lax.rem(dp + k, 16)
-            pltpu.make_async_remote_copy(
-                piece(d), st1[t].at[dp], m1s.at[t], m1r.at[t],
-                device_id={"dp": d}, device_id_type=MESH,
-            ).start()
+        for k in range(16):
+            piece = modv.at[pl.ds(piece_rows[k], 16), pl.ds(t * CW + piece_cols[k], PW)]
+            if k == 0:
+                pltpu.make_async_copy(piece, st1[t].at[dp], m1r.at[t]).start()
+            else:
+                pltpu.make_async_remote_copy(
+                    piece, st1[t].at[dp], m1s.at[t], m1r.at[t],
+                    device_id={"dp": groups[k]}, device_id_type=MESH,
+                ).start()
 
     def send_m2(t):
         pltpu.make_async_copy(st1[t], st1[t], m1r.at[t]).wait()
-
-        @pl.loop(0, 16)
-        def _(d):
-            st2[t, d] = st1[t][anchor_of(mv, sq, d)]
-
+        for d in range(16):
+            st2[t, d] = st1[t][anchors[d]]
         place = gath.at[
-            pl.ds(aligned(sq * RB + dp // 2 * 16, 16), 16),
-            pl.ds(aligned(t * CW + dp % 2 * PW, PW), PW),
+            pl.ds(aligned(sq * RB + piece_rows[0], 16), 16), pl.ds(t * CW + piece_cols[0], PW)
         ]
         pltpu.make_async_copy(st2.at[t, dp], place, m2r.at[t]).start()
-
-        @pl.loop(1, 16)
-        def _(k):
-            d = lax.rem(dp + k, 16)
+        for k in range(1, 16):
             pltpu.make_async_remote_copy(
-                st2.at[t, d], place, m2s.at[t], m2r.at[t],
-                device_id={"dp": d}, device_id_type=MESH,
+                st2.at[t, groups[k]], place, m2s.at[t], m2r.at[t],
+                device_id={"dp": groups[k]}, device_id_type=MESH,
             ).start()
 
-    def column(h, i, j):
+    def base(h, i, j):
         if h == 0:
-            return lax.rem(y + j + 4, 4) * 4 + lax.rem(x + i + 4, 4)
-        return lax.rem(y + i + 4, 4) * 4 + lax.rem(x + j + 4, 4)
+            return bases[j % 4][i % 4]
+        return bases[i % 4][j % 4]
 
     def beside(along_x, step):
         if along_x:
-            return {"seq": y * 4 + lax.rem(x + step + 4, 4)}
-        return {"seq": lax.rem(y + step + 4, 4) * 4 + x}
+            return {"seq": ys[0] * 4 + xs[step % 4]}
+        return {"seq": ys[step % 4] * 4 + xs[0]}
 
     def region(t, h, i, j, part):
-        low = column(h, i, j) * RB + h * HALF + (QUART if part == 2 else 0)
+        low = base(h, i, j) + h * HALF + (QUART if part == 2 else 0)
         count = HALF if part == 0 else QUART
         return gath.at[pl.ds(aligned(low, QUART), count), pl.ds(t * CW, CW)]
 
@@ -182,7 +177,7 @@
         i, j, _, _, part, along_x, step = event(t, h, e)
         place = region(t, h, i, j, part)
         pltpu.make_async_remote_copy(
-            place, place, gs.at[t, h, e], gr.at[t, h, e],
+            place, place, gs.at[t], gf.at[t] if e in LAST else gr.at[t, h, e],
             device_id=beside(along_x, step), device_id_type=MESH,
         ).start()
 
@@ -190,11 +185,6 @@
         _, _, gi, gj, part, _, _ = event(t, h, e)
         place = region(t, h, gi, gj, part)
         pltpu.make_async_copy(place, place, gr.at[t, h, e]).wait()
-
-    def sent(t, h, e):
-        i, j, _, _, part, _, _ = event(t, h, e)
-        place = region(t, h, i, j, part)
-        pltpu.make_async_copy(place, place, gs.at[t, h, e]).wait()
 
     def stage2(t):
         place = gath.at[pl.ds(aligned(sq * RB, RB), RB), pl.ds(t * CW, CW)]
@@ -236,10 +226,8 @@
                 put(t, h, 18 + kind)
 
     def stage6(t):
-        for h in (0, 1):
-            for k in range(4):
-                got(t, h, 6 + 4 * k)
-                got(t, h, 7 + 4 * k)
+        place = gath.at[pl.ds(0, 16 * QUART), pl.ds(t * CW, CW)]
+        pltpu.make_async_copy(place, place, gf.at[t]).wait()
         pltpu.make_async_copy(
             gath.at[:, pl.ds(t * CW, CW)], gout.at[:, pl.ds(t * CW, CW)], ls.at[t]
         ).start()
@@ -303,7 +291,6 @@
 
     send_m1(0)
     send_cot()
-    send_m1(1)
     stages = ((5, stage5), (4, stage4), (3, stage3), (2, stage2))
     for n in range(CHUNKS + 5):
         for s, run in stages:
@@ -312,15 +299,16 @@
                 run(t)
         if n < CHUNKS:
             send_m2(n)
+        if n == 0:
+            send_m1(1)
         if n + 2 < CHUNKS:
             send_m1(n + 2)
         if n <= 4:
             weights(n)
         if n == 5:
             weights_end()
-        t = n - 5
-        if 0 <= t < CHUNKS:
-            stage6(t)
+        if 0 <= n - 5 < CHUNKS:
+            stage6(n - 5)
 
     pltpu.make_async_copy(up, up, cr).wait()
     part = up.at[pl.ds(0, 15 * RB), :]
@@ -329,9 +317,8 @@
         part = st1[t].at[pl.ds(0, 15)]
         pltpu.make_async_copy(part, part, m1s.at[t]).wait()
         pltpu.make_async_copy(part, part, m2s.at[t]).wait()
-        for h in (0, 1):
-            for e in range(20):
-                sent(t, h, e)
+        part = gath.at[pl.ds(0, 20 * (HALF + QUART)), pl.ds(t * CW, CW)]
+        pltpu.make_async_copy(part, part, gs.at[t]).wait()
         pltpu.make_async_copy(
             gath.at[:, pl.ds(t * CW, CW)], gout.at[:, pl.ds(t * CW, CW)], ls.at[t]
         ).wait()
@@ -366,7 +353,7 @@
             pltpu.VMEM((GR, D), BF16),
             pltpu.VMEM((D, 3 * DH), BF16),
             dma((CHUNKS,)), dma((CHUNKS,)), dma((CHUNKS,)), dma((CHUNKS,)),
-            dma((CHUNKS, 2, 20)), dma((CHUNKS, 2, 20)),
+            dma((CHUNKS,)), dma((CHUNKS, 2, 20)), dma((CHUNKS,)),
             dma((4,)), dma((4,)), dma((3,)), dma((3,)), dma((8,)), dma((8,)), dma(()),
             dma(()), dma(()), dma((CHUNKS,)),
         ],
@@ -377,12 +364,17 @@
 
 
 MASK = 4096.0
+TQ = 2 * RB
+TK = 4 * RB
+NQ = GR // TQ
+NK = GR // TK
+SLOTS = NQ * NK + 6
 
 
 def attention_kernel(
     img, mv, proj, up, gain,
     att, hg,
-    qx, kx, vx, ux, us, es, dq, dk, dv, place, back, low, high,
+    qx, kx, vx, ux, us, es, sa, sb, da, db, oa, dq, dk, dv, place, back, low, high, lq, lk,
 ):
     group = lax.axis_index("dp")
     scale = 1.0 / math.sqrt(DH)
@@ -392,30 +384,58 @@
         slot = jnp.int32(0)
         end = jnp.int32(0)
         for i in range(8):
-            end = end + img[anchor, i]
+            end = end + img[i, anchor]
             slot = slot + (c * RB >= end).astype(jnp.int32)
         segs.append(anchor * 8 + slot)
+    same = [jnp.int32(1)] * NC
+    ahead = [jnp.int32(0)] * NC
     for c in range(NC):
-        less = jnp.int32(0)
-        same = jnp.int32(0)
-        ahead = jnp.int32(0)
-        for o in range(NC):
-            less = less + (segs[o] < segs[c]).astype(jnp.int32)
+        for o in range(c):
             equal = (segs[o] == segs[c]).astype(jnp.int32)
-            same = same + equal
-            if o < c:
-                ahead = ahead + equal
-        spot = less + ahead
+            same[c] = same[c] + equal
+            same[o] = same[o] + equal
+            ahead[c] = ahead[c] + equal
+    keys = [(NC - same[c]) * 256 + segs[c] for c in range(NC)]
+    less = [jnp.int32(0)] * NC
+    for c in range(NC):
+        for o in range(c):
+            below = (keys[o] < keys[c]).astype(jnp.int32)
+            above = (keys[o] > keys[c]).astype(jnp.int32)
+            less[c] = less[c] + below
+            less[o] = less[o] + above
+    for c in range(NC):
+        spot = less[c] + ahead[c]
         place[c] = spot
         back[spot] = c
-        low[spot] = less
-        high[spot] = less + same
+        low[spot] = less[c]
+        high[spot] = less[c] + same[c]
+
+    for i in range(2):
+        lq[i] = NQ
+        lk[i] = NK
+
+    def list_row(qt, n):
+        first = low[qt * (TQ // RB)] // (TK // RB)
+        last = (high[qt * (TQ // RB) + TQ // RB - 1] + TK // RB - 1) // (TK // RB)
+
+        def one(kt, n):
+            lq[n] = qt
+            lk[n] = kt
+            return n + 1
+
+        return lax.fori_loop(first, last, one, n)
+
+    count = lax.fori_loop(0, NQ, list_row, jnp.int32(2))
+    for i in range(4):
+        lq[count + i] = NQ
+        lk[count + i] = NK
+    steps = (count + 1) // 2
 
     lanes = lax.broadcasted_iota(jnp.int32, (RB, DH), 1)
     gain_q = gain[0:1, :]
     gain_k = gain[1:2, :]
 
-    @pl.loop(0, NC)
+    @pl.loop(0, NC, unroll=4)
     def _(c):
         r0 = aligned(c * RB, RB)
         spot = place[c]
@@ -432,63 +452,63 @@
         tail = lanes == NC
         qx[pl.ds(s0, RB), DH:] = jnp.where(hot, MASK, jnp.where(tail, 1.0, 0.0)).astype(BF16)
         kx[pl.ds(s0, RB), DH:] = jnp.where(hot, 1.0, jnp.where(tail, -MASK, 0.0)).astype(BF16)
-        vx[pl.ds(s0, RB), DH:] = jnp.where(lanes < 2, -1.0, 0.0).astype(BF16)
+        vx[pl.ds(s0, RB), DH:] = jnp.full((RB, DH), -1.0, BF16)
         us[pl.ds(s0, RB), :] = up[pl.ds(r0, RB), :]
 
+    oa[...] = jnp.zeros_like(oa)
+    dq[...] = jnp.zeros_like(dq)
     dk[...] = jnp.zeros_like(dk)
     dv[...] = jnp.zeros_like(dv)
-    wide = lax.broadcasted_iota(jnp.int32, (2 * RB, DH), 1)
     factor = scale * math.log2(math.e)
 
-    @pl.loop(0, NC // 2)
-    def _(qt):
-        q0 = aligned(qt * 2 * RB, 2 * RB)
-        first = low[2 * qt] // 2
-        last = (high[2 * qt + 1] + 1) // 2
-        q_tile = qx[pl.ds(q0, 2 * RB), :]
-
-        def forward(kt, total):
-            k0 = aligned(kt * 2 * RB, 2 * RB)
-            scores = lax.dot_general(
-                q_tile, kx[pl.ds(k0, 2 * RB), :], NT, preferred_element_type=F32
-            )
-            e = jnp.exp2(scores * factor).astype(BF16)
-            es[kt] = e
-            return total + jnp.dot(e, vx[pl.ds(k0, 2 * RB), :], preferred_element_type=F32)
-
-        total = lax.fori_loop(first, last, forward, jnp.zeros((2 * RB, 2 * DH), F32))
-        inverse = -1.0 / total[:, DH : DH + 1]
-        out = (total[:, :DH] * inverse).astype(BF16)
-        for b in range(2):
-            att[pl.ds(aligned(back[2 * qt + b] * RB, RB), RB), :] = out[b * RB : (b + 1) * RB]
-        u = us[pl.ds(q0, 2 * RB), :].astype(F32)
-        delta = jnp.sum(u * out.astype(F32), axis=1, keepdims=True) * inverse
-        coarse = delta.astype(BF16).astype(F32)
-        fine = delta - coarse
-        u_tile = (u * inverse).astype(BF16)
-        ux[:, :DH] = u_tile
-        ux[:, DH:] = jnp.where(wide == 0, coarse, jnp.where(wide == 1, fine, 0.0)).astype(BF16)
-
-        def backward(kt, grad):
-            k0 = aligned(kt * 2 * RB, 2 * RB)
-            e = es[kt]
-            inner = lax.dot_general(
-                ux[...], vx[pl.ds(k0, 2 * RB), :], NT, preferred_element_type=F32
-            )
-            ds = (e.astype(F32) * inner).astype(BF16)
-            dv[pl.ds(k0, 2 * RB), :] += lax.dot_general(
-                e, ux[:, :DH], TN, preferred_element_type=F32
-            )
-            dk[pl.ds(k0, 2 * RB), :] += lax.dot_general(
-                ds, qx[pl.ds(q0, 2 * RB), :DH], TN, preferred_element_type=F32
-            )
-            return grad + jnp.dot(ds, kx[pl.ds(k0, 2 * RB), :DH], preferred_element_type=F32)
-
-        dq[pl.ds(q0, 2 * RB), :] = lax.fori_loop(
-            first, last, backward, jnp.zeros((2 * RB, DH), F32)
-        )
-
-    @pl.loop(0, NC)
+    def rows_q(i):
+        return pl.ds(aligned(lq[i] * TQ, TQ), TQ)
+
+    def rows_k(i):
+        return pl.ds(aligned(lk[i] * TK, TK), TK)
+
+    def forward(i, mine, other):
+        oa[rows_q(i), :] += jnp.dot(es[i], vx[rows_k(i), :], preferred_element_type=F32)
+        es[i + 1] = jnp.exp2(other[...] * factor).astype(BF16)
+        mine[...] = lax.dot_general(
+            qx[rows_q(i + 2), :], kx[rows_k(i + 2), :], NT, preferred_element_type=F32
+        )
+
+    @pl.loop(0, steps)
+    def _(j):
+        forward(2 * j, sa, sb)
+        forward(2 * j + 1, sb, sa)
+
+    @pl.loop(0, NC, unroll=4)
+    def _(b):
+        s0 = aligned(b * RB, RB)
+        inverse = -1.0 / oa[pl.ds(s0, RB), DH:]
+        out = (oa[pl.ds(s0, RB), :DH] * inverse).astype(BF16)
+        att[pl.ds(aligned(back[b] * RB, RB), RB), :] = out
+        scaled = us[pl.ds(s0, RB), :].astype(F32) * inverse
+        ux[pl.ds(s0, RB), :DH] = scaled.astype(BF16)
+        ux[pl.ds(s0, RB), DH:] = (scaled * out.astype(F32)).astype(BF16)
+
+    def backward(i, mine, other, ds_mine, ds_other):
+        q_rows = rows_q(i)
+        k_rows = rows_k(i)
+        dv[k_rows, :] += lax.dot_general(
+            es[i], ux[q_rows, :DH], TN, preferred_element_type=F32
+        )
+        ds = ds_other[...]
+        dk[k_rows, :] += lax.dot_general(ds, qx[q_rows, :DH], TN, preferred_element_type=F32)
+        dq[q_rows, :] += jnp.dot(ds, kx[k_rows, :DH], preferred_element_type=F32)
+        ds_mine[...] = (es[i + 1].astype(F32) * other[...]).astype(BF16)
+        mine[...] = lax.dot_general(
+            ux[rows_q(i + 2), :], vx[rows_k(i + 2), :], NT, preferred_element_type=F32
+        )
+
+    @pl.loop(0, steps)
+    def _(j):
+        backward(2 * j, sa, sb, da, db)
+        backward(2 * j + 1, sb, sa, db, da)
+
+    @pl.loop(0, NC, unroll=4)
     def _(c):
         r0 = aligned(c * RB, RB)
         s0 = aligned(place[c] * RB, RB)
@@ -521,19 +541,26 @@
         in_specs=[smem, smem, vmem, vmem, vmem],
         out_specs=(vmem, vmem),
         scratch_shapes=[
-            pltpu.VMEM((GR, 2 * DH), BF16),
-            pltpu.VMEM((GR, 2 * DH), BF16),
-            pltpu.VMEM((GR, 2 * DH), BF16),
-            pltpu.VMEM((2 * RB, 2 * DH), BF16),
+            pltpu.VMEM((GR + TQ, 2 * DH), BF16),
+            pltpu.VMEM((GR + TK, 2 * DH), BF16),
+            pltpu.VMEM((GR + TK, 2 * DH), BF16),
+            pltpu.VMEM((GR + TQ, 2 * DH), BF16),
             pltpu.VMEM((GR, DH), BF16),
-            pltpu.VMEM((NC // 2, 2 * RB, 2 * RB), BF16),
-            pltpu.VMEM((GR, DH), F32),
-            pltpu.VMEM((GR, DH), F32),
-            pltpu.VMEM((GR, DH), F32),
+            pltpu.VMEM((SLOTS, TQ, TK), BF16),
+            pltpu.VMEM((TQ, TK), F32),
+            pltpu.VMEM((TQ, TK), F32),
+            pltpu.VMEM((TQ, TK), BF16),
+            pltpu.VMEM((TQ, TK), BF16),
+            pltpu.VMEM((GR + TQ, 2 * DH), F32),
+            pltpu.VMEM((GR + TQ, DH), F32),
+            pltpu.VMEM((GR + TK, DH), F32),
+            pltpu.VMEM((GR + TK, DH), F32),
             pltpu.SMEM((NC,), jnp.int32),
             pltpu.SMEM((NC,), jnp.int32),
             pltpu.SMEM((NC,), jnp.int32),
             pltpu.SMEM((NC,), jnp.int32),
+            pltpu.SMEM((SLOTS,), jnp.int32),
+            pltpu.SMEM((SLOTS,), jnp.int32),
         ],
         compiler_params=pltpu.CompilerParams(vmem_limit_bytes=VMEM_LIMIT),
     )(img, mv, proj, up, gain)
@@ -541,6 +568,7 @@
 
 STEPS = (2, 3, 1, 0)
 FC = 4 * SHARD
+PART = SHARD // 2
 
 
 def reduce_kernel(
@@ -563,14 +591,16 @@
             rows.at[:, pl.ds(aligned(chunk(n) * FC, 128), FC)], xs.at[n], xsem.at[n]
         )
 
-    for n in range(4):
-        load(n).start()
+    load(0).start()
+    load(1).start()
     barrier = pltpu.get_barrier_semaphore()
     for device in (other, to_z(1), to_z(-1)):
         pl.semaphore_signal(barrier, inc=1, device_id=device, device_id_type=MESH)
 
     def compute(n):
         load(n).wait()
+        if n < 2:
+            load(n + 2).start()
         m = chunk(n)
         dw[m] = lax.dot_general(xs[n], hg[...], TN, preferred_element_type=F32)
 
@@ -590,36 +620,40 @@
         for j in range(2):
             pair_copy(n, j).wait_recv()
 
-    def part(dz):
+    def part(dz, b):
         zz = lax.rem(z + dz + 8, 8)
-        at = aligned((lax.rem(zz, 2) * 2 + core) * SHARD, 16)
-        return dw[zz // 2, pl.ds(at, SHARD), :] + pair[zz]
-
-    def up_copy(k):
+        at = aligned((lax.rem(zz, 2) * 2 + core) * SHARD + b * PART, 16)
+        return dw[zz // 2, pl.ds(at, PART), :] + pair[zz, pl.ds(b * PART, PART), :]
+
+    def up_copy(k, b):
         return pltpu.make_async_remote_copy(
-            su.at[k], ru.at[k], us.at[k], ur.at[k], device_id=to_z(1), device_id_type=MESH
-        )
-
-    def down_copy(k):
+            su.at[k, b], ru.at[k, b], us.at[k, b], ur.at[k, b],
+            device_id=to_z(1), device_id_type=MESH,
+        )
+
+    def down_copy(k, b):
         return pltpu.make_async_remote_copy(
-            sd.at[k], rd.at[k], ds.at[k], dr.at[k], device_id=to_z(-1), device_id_type=MESH
+            sd.at[k, b], rd.at[k, b], ds.at[k, b], dr.at[k, b],
+            device_id=to_z(-1), device_id_type=MESH,
         )
 
     def go_up(k):
-        value = part(4 - k)
-        if k:
-            up_copy(k - 1).wait_recv()
-            value = value + ru[k - 1].astype(F32)
-        su[k] = value.astype(BF16)
-        up_copy(k).start()
+        for b in range(2):
+            value = part(4 - k, b)
+            if k:
+                up_copy(k - 1, b).wait_recv()
+                value = value + ru[k - 1, b].astype(F32)
+            su[k, b] = value.astype(BF16)
+            up_copy(k, b).start()
 
     def go_down(k):
-        value = part(k - 3)
-        if k:
-            down_copy(k - 1).wait_recv()
-            value = value + rd[k - 1].astype(F32)
-        sd[k] = value.astype(BF16)
-        down_copy(k).start()
+        for b in range(2):
+            value = part(k - 3, b)
+            if k:
+                down_copy(k - 1, b).wait_recv()
+                value = value + rd[k - 1, b].astype(F32)
+            sd[k, b] = value.astype(BF16)
+            down_copy(k, b).start()
 
     compute(0)
     pl.semaphore_wait(barrier, 3)
@@ -641,18 +675,20 @@
     pair_wait(3)
     go_down(2)
     go_up(3)
-    total = part(0)
-    down_copy(2).wait_recv()
-    total = total + rd[2].astype(F32)
-    up_copy(3).wait_recv()
-    grad[...] = total + ru[3].astype(F32)
+    for b in range(2):
+        total = part(0, b)
+        down_copy(2, b).wait_recv()
+        total = total + rd[2, b].astype(F32)
+        up_copy(3, b).wait_recv()
+        grad[b * PART : (b + 1) * PART, :] = total + ru[3, b].astype(F32)
     for n in range(4):
         for j in range(2):
             pair_copy(n, j).wait_send()
-    for k in range(4):
-        up_copy(k).wait_send()
-    for k in range(3):
-        down_copy(k).wait_send()
+    for b in range(2):
+        for k in range(4):
+            up_copy(k, b).wait_send()
+        for k in range(3):
+            down_copy(k, b).wait_send()
 
 
 def reduce_call(rows, hg):
@@ -670,11 +706,12 @@
             pltpu.VMEM((4, GR, FC), BF16),
             pltpu.VMEM((4, FC, wide), F32),
             pltpu.VMEM((8, SHARD, wide), F32),
-            pltpu.VMEM((4, SHARD, wide), BF16),
-            pltpu.VMEM((4, SHARD, wide), BF16),
-            pltpu.VMEM((3, SHARD, wide), BF16),
-            pltpu.VMEM((3, SHARD, wide), BF16),
-            dma((4,)), dma((4, 2)), dma((4, 2)), dma((4,)), dma((4,)), dma((3,)), dma((3,)),
+            pltpu.VMEM((4, 2, PART, wide), BF16),
+            pltpu.VMEM((4, 2, PART, wide), BF16),
+            pltpu.VMEM((3, 2, PART, wide), BF16),
+            pltpu.VMEM((3, 2, PART, wide), BF16),
+            dma((4,)), dma((4, 2)), dma((4, 2)),
+            dma((4, 2)), dma((4, 2)), dma((3, 2)), dma((3, 2)),
         ],
         compiler_params=pltpu.CompilerParams(
             collective_id=1, has_side_effects=True, vmem_limit_bytes=VMEM_LIMIT
@@ -683,11 +720,12 @@
 
 
 def body(tokens, modulation, img_size, text_count, move_list, w_qkv, qk_gain, cotangent):
-    moves = move_list.reshape(NC, 8)
+    moves = move_list.transpose(1, 2, 0)
+    sizes = img_size.T
     gathered, projected, upstream = gather_call(
-        img_size, text_count, moves, tokens, modulation, w_qkv, cotangent
+        sizes, text_count.T, moves, tokens, modulation, w_qkv, cotangent
     )
-    attended, head_grads = attention_call(img_size, moves, projected, upstream, qk_gain)
+    attended, head_grads = attention_call(sizes, moves, projected, upstream, qk_gain)
     return (attended, reduce_call(gathered, head_grads))
 
 

time: 179 us -> 146 us (0.82)
  Pallas kernels: 171 us -> 143 us
  local copies, waits for them, and re-layouts: 5.71 us -> 1.65 us
    pallas_call x1, Pallas kernels: 57.8 us -> 36.1 us  [reduce_call(): pl.pallas_call(reduce_kernel, name='grad_reduce', out_shape=jax.ShapeDtyp...]
    pallas_call x1, Pallas kernels: 21.9 us -> 15 us  [attention_call(): pl.pallas_call(attention_kernel, name='attention', out_shape=(jax.ShapeDt...]
    unnamed x3 -> x1, local copies, waits for them, and re-layouts: 4.36 us -> 1.65 us
where the time goes in v2:
time: 146 us; the launch traced here: 145 us
  Pallas kernels  143 us (98%)
  local copies, waits for them, and re-layouts  1.65 us (1%)
    pallas_call x1, Pallas kernels, gather_call(): pl.pallas_call(gather_kernel, name='gather_project', out_shape=(jax.Shape...  91.6 us
    pallas_call x1, Pallas kernels, reduce_call(): pl.pallas_call(reduce_kernel, name='grad_reduce', out_shape=jax.ShapeDtyp...  36.1 us
    pallas_call x1, Pallas kernels, attention_call(): pl.pallas_call(attention_kernel, name='attention', out_shape=(jax.ShapeDt...  15 us

profile of v2, /device:TPU:2, one launch (start us, length us, event | category | flops | bytes accessed | tf_op | source)
XLA Modules:
  0.0 145.0 jit_solution(6411101714082762493)
XLA Ops:
  0.6 91.6 %gather_project.1 = (bf16[2048,2560]{1,0:T(8,128)(2,1)}, f32[2048,384]{1,0:T(8,128)}, bf16[2048,128]{1,0:T(8,128)(2,1)}) custom-call(s32[8,16]{1,0:T(8,128)} %bitcast.3, s32[8,16]{1,0:T(8,128)} %bitcast.7, s32[4,2,16]{2,1,0:T(2,128)} %bitcast.5, bf16[128,2560]{1,0:T(8,128)(2,1)} %tok.1, f32[4,8,2560]{2,1,0:T(8,128)} %mod.1, bf16[160,384]{1,0:T(8,128)(2,1)} %w.1, ...), custom_call_target="tpu_custom_call" | custom-call | tf_op jit(solution)/shard_map/gather_project/pallas_call | solution.py:339
  92.2 15.0 %attention.1 = (bf16[2048,128]{1,0:T(8,128)(2,1)}, bf16[2048,384]{1,0:T(8,128)(2,1)}) custom-call(s32[8,16]{1,0:T(8,128)} %bitcast.4, s32[4,2,16]{2,1,0:T(2,128)} %bitcast.6, f32[2048,384]{1,0:T(8,128)} %get-tuple-element.7.proj, bf16[2048,128]{1,0:T(8,128)(2,1)} %get-tuple-element.8.up, f32[2,128]{1,0:T(2,128)} %gain.1), custom_call_target="tpu_custom_call" | custom-call | tf_op jit(solution)/shard_map/attention/pallas_call | solution.py:534
  107.2 36.1 %grad_reduce.1 = f32[160,384]{1,0:T(8,128)} custom-call(bf16[2048,2560]{1,0:T(8,128)(2,1)} %get-tuple-element.10.rows, bf16[2048,384]{1,0:T(8,128)(2,1)} %get-tuple-element.11.hg), custom_call_target="tpu_custom_call" | custom-call | tf_op jit(solution)/shard_map/grad_reduce/pallas_call | solution.py:699
  143.3 1.7 %copy.11 = f32[160,384]{1,0:T(8,128)} copy(f32[160,384]{1,0:T(8,128)} %grad_reduce.1) | data formatting | bytes 491520

commit v3 on v2

--- a/solution.py
+++ b/solution.py
@@ -41,10 +41,14 @@
 
 
 def gather_kernel(
-    img, txt, mv, tok, mod, w, cot,
-    gout, proj, up,
-    modv, *scratch,
+    img, txt, mv, tok_in, mod_in, w, cot,
+    gout, proj_out, up,
+    tok, mod, proj, modv, load_sems, proj_sem, *scratch,
 ):
+    load_tok = pltpu.make_async_copy(tok_in, tok, load_sems.at[0])
+    load_mod = pltpu.make_async_copy(mod_in, mod, load_sems.at[1])
+    load_tok.start()
+    load_mod.start()
     st1 = scratch[:CHUNKS]
     st2, gath, wfull, m1s, m1r, m2s, m2r, gs, gr, gf, *scratch = scratch[CHUNKS:]
     wus, wur, wds, wdr, wss, wsr, wl, cs, cr, ls = scratch
@@ -82,6 +86,9 @@
         start = jnp.where(hit, end, start)
     slot = jnp.minimum(slot, 7)
     limit = txt[slot, dp] - (first - start)
+
+    load_tok.wait()
+    load_mod.wait()
 
     @pl.loop(0, RB // 16)
     def _(i):
@@ -244,6 +251,10 @@
                 proj[pl.ds(r0, 256), :] = term
             else:
                 proj[pl.ds(r0, 256), :] += term
+            if t == CHUNKS - 1:
+                pltpu.make_async_copy(
+                    proj.at[pl.ds(r0, 256), :], proj_out.at[pl.ds(r0, 256), :], proj_sem
+                ).start()
 
     def shard(dz, c):
         return wfull.at[pl.ds(aligned((lax.rem(z + dz + 8, 8) * 2 + c) * SHARD, 16), SHARD), :]
@@ -322,6 +333,7 @@
         pltpu.make_async_copy(
             gath.at[:, pl.ds(t * CW, CW)], gout.at[:, pl.ds(t * CW, CW)], ls.at[t]
         ).wait()
+    pltpu.make_async_copy(proj, proj_out, proj_sem).wait()
     own = shard(0, core)
     for k in range(4):
         w_got(own, wus.at[k])
@@ -332,7 +344,6 @@
 
 
 def gather_call(img, txt, mv, tok, mod, w, cot):
-    vmem = pl.BlockSpec(memory_space=pltpu.VMEM)
     smem = pl.BlockSpec(memory_space=pltpu.SMEM)
     hbm = pl.BlockSpec(memory_space=pl.ANY)
     dma = pltpu.SemaphoreType.DMA
@@ -344,10 +355,14 @@
             jax.ShapeDtypeStruct((GR, 3 * DH), F32),
             jax.ShapeDtypeStruct((GR, DH), BF16),
         ),
-        in_specs=[smem, smem, smem, vmem, vmem, hbm, hbm],
-        out_specs=(hbm, vmem, hbm),
+        in_specs=[smem, smem, smem, hbm, hbm, hbm, hbm],
+        out_specs=(hbm, hbm, hbm),
         scratch_shapes=[
             pltpu.VMEM((RB, D), BF16),
+            pltpu.VMEM((4, 8, D), F32),
+            pltpu.VMEM((GR, 3 * DH), F32),
+            pltpu.VMEM((RB, D), BF16),
+            dma((2,)), dma(()),
             *[pltpu.VMEM((16, 16, PW), BF16)] * CHUNKS,
             pltpu.VMEM((CHUNKS, 16, 16, PW), BF16),
             pltpu.VMEM((GR, D), BF16),
@@ -364,18 +379,31 @@
 
 
 MASK = 4096.0
-TQ = 2 * RB
+TQ = 4 * RB
 TK = 4 * RB
 NQ = GR // TQ
 NK = GR // TK
 SLOTS = NQ * NK + 6
+PIECES = 4
+PIECE = GR // PIECES
 
 
 def attention_kernel(
-    img, mv, proj, up, gain,
-    att, hg,
+    img, mv, proj_in, up_in, gain,
+    att_out, hg_out,
+    proj, up, att, hg,
     qx, kx, vx, ux, us, es, sa, sb, da, db, oa, dq, dk, dv, place, back, low, high, lq, lk,
+    sems, out_sem,
 ):
+    def load(part):
+        rows = pl.ds(part * PIECE, PIECE)
+        return pltpu.make_async_copy(proj_in.at[rows, :], proj.at[rows, :], sems.at[part])
+
+    load_up = pltpu.make_async_copy(up_in, up, sems.at[PIECES])
+    load(0).start()
+    load_up.start()
+    for part in range(1, PIECES):
+        load(part).start()
     group = lax.axis_index("dp")
     scale = 1.0 / math.sqrt(DH)
     segs = []
@@ -435,8 +463,7 @@
     gain_q = gain[0:1, :]
     gain_k = gain[1:2, :]
 
-    @pl.loop(0, NC, unroll=4)
-    def _(c):
+    def prepare(c):
         r0 = aligned(c * RB, RB)
         spot = place[c]
         s0 = aligned(spot * RB, RB)
@@ -455,6 +482,12 @@
         vx[pl.ds(s0, RB), DH:] = jnp.full((RB, DH), -1.0, BF16)
         us[pl.ds(s0, RB), :] = up[pl.ds(r0, RB), :]
 
+    load_up.wait()
+    for part in range(PIECES):
+        load(part).wait()
+        for c in range(part * NC // PIECES, (part + 1) * NC // PIECES):
+            prepare(c)
+
     oa[...] = jnp.zeros_like(oa)
     dq[...] = jnp.zeros_like(dq)
     dk[...] = jnp.zeros_like(dk)
@@ -489,6 +522,9 @@
         ux[pl.ds(s0, RB), :DH] = scaled.astype(BF16)
         ux[pl.ds(s0, RB), DH:] = (scaled * out.astype(F32)).astype(BF16)
 
+    att_copy = pltpu.make_async_copy(att, att_out, out_sem.at[0])
+    att_copy.start()
+
     def backward(i, mine, other, ds_mine, ds_other):
         q_rows = rows_q(i)
         k_rows = rows_k(i)
@@ -508,8 +544,7 @@
         backward(2 * j, sa, sb, da, db)
         backward(2 * j + 1, sb, sa, db, da)
 
-    @pl.loop(0, NC, unroll=4)
-    def _(c):
+    def finish(c):
         r0 = aligned(c * RB, RB)
         s0 = aligned(place[c] * RB, RB)
 
@@ -527,9 +562,22 @@
         ).astype(BF16)
         hg[pl.ds(r0, RB), 2 * DH :] = dv[pl.ds(s0, RB), :].astype(BF16)
 
+    def store(part):
+        rows = pl.ds(part * PIECE, PIECE)
+        return pltpu.make_async_copy(hg.at[rows, :], hg_out.at[rows, :], out_sem.at[part + 1])
+
+    for part in range(PIECES):
+        for c in range(part * NC // PIECES, (part + 1) * NC // PIECES):
+            finish(c)
+        store(part).start()
+    att_copy.wait()
+    for part in range(PIECES):
+        store(part).wait()
+
 
 def attention_call(img, mv, proj, up, gain):
     vmem = pl.BlockSpec(memory_space=pltpu.VMEM)
+    hbm = pl.BlockSpec(memory_space=pl.ANY)
     smem = pl.BlockSpec(memory_space=pltpu.SMEM)
     return pl.pallas_call(
         attention_kernel,
@@ -538,9 +586,13 @@
             jax.ShapeDtypeStruct((GR, DH), BF16),
             jax.ShapeDtypeStruct((GR, 3 * DH), BF16),
         ),
-        in_specs=[smem, smem, vmem, vmem, vmem],
-        out_specs=(vmem, vmem),
+        in_specs=[smem, smem, hbm, hbm, vmem],
+        out_specs=(hbm, hbm),
         scratch_shapes=[
+            pltpu.VMEM((GR, 3 * DH), F32),
+            pltpu.VMEM((GR, DH), BF16),
+            pltpu.VMEM((GR, DH), BF16),
+            pltpu.VMEM((GR, 3 * DH), BF16),
             pltpu.VMEM((GR + TQ, 2 * DH), BF16),
             pltpu.VMEM((GR + TK, 2 * DH), BF16),
             pltpu.VMEM((GR + TK, 2 * DH), BF16),
@@ -561,6 +613,8 @@
             pltpu.SMEM((NC,), jnp.int32),
             pltpu.SMEM((SLOTS,), jnp.int32),
             pltpu.SMEM((SLOTS,), jnp.int32),
+            pltpu.SemaphoreType.DMA((PIECES + 1,)),
+            pltpu.SemaphoreType.DMA((PIECES + 1,)),
         ],
         compiler_params=pltpu.CompilerParams(vmem_limit_bytes=VMEM_LIMIT),
     )(img, mv, proj, up, gain)
@@ -569,11 +623,13 @@
 STEPS = (2, 3, 1, 0)
 FC = 4 * SHARD
 PART = SHARD // 2
+UP = (4, 3)
+DOWN = (3, 4)
 
 
 def reduce_kernel(
-    rows, hg, grad,
-    xs, dw, pair, su, ru, sd, rd,
+    rows, hg_in, grad,
+    hg, hg_sem, xs, dw, pair, su, ru, sd, rd,
     xsem, ps, pr, us, ur, ds, dr,
 ):
     dp = lax.axis_index("dp")
@@ -591,16 +647,21 @@
             rows.at[:, pl.ds(aligned(chunk(n) * FC, 128), FC)], xs.at[n], xsem.at[n]
         )
 
+    load_hg = pltpu.make_async_copy(hg_in, hg, hg_sem)
     load(0).start()
-    load(1).start()
+    load_hg.start()
     barrier = pltpu.get_barrier_semaphore()
     for device in (other, to_z(1), to_z(-1)):
         pl.semaphore_signal(barrier, inc=1, device_id=device, device_id_type=MESH)
 
     def compute(n):
         load(n).wait()
-        if n < 2:
-            load(n + 2).start()
+        if n == 0:
+            load(1).start()
+            load(2).start()
+            load_hg.wait()
+        if n == 1:
+            load(3).start()
         m = chunk(n)
         dw[m] = lax.dot_general(xs[n], hg[...], TN, preferred_element_type=F32)
 
@@ -637,23 +698,21 @@
             device_id=to_z(-1), device_id_type=MESH,
         )
 
-    def go_up(k):
-        for b in range(2):
-            value = part(4 - k, b)
-            if k:
-                up_copy(k - 1, b).wait_recv()
-                value = value + ru[k - 1, b].astype(F32)
-            su[k, b] = value.astype(BF16)
-            up_copy(k, b).start()
-
-    def go_down(k):
-        for b in range(2):
-            value = part(k - 3, b)
-            if k:
-                down_copy(k - 1, b).wait_recv()
-                value = value + rd[k - 1, b].astype(F32)
-            sd[k, b] = value.astype(BF16)
-            down_copy(k, b).start()
+    def go_up(k, b):
+        value = part(UP[b] - k, b)
+        if k:
+            up_copy(k - 1, b).wait_recv()
+            value = value + ru[k - 1, b].astype(F32)
+        su[k, b] = value.astype(BF16)
+        up_copy(k, b).start()
+
+    def go_down(k, b):
+        value = part(k - DOWN[b], b)
+        if k:
+            down_copy(k - 1, b).wait_recv()
+            value = value + rd[k - 1, b].astype(F32)
+        sd[k, b] = value.astype(BF16)
+        down_copy(k, b).start()
 
     compute(0)
     pl.semaphore_wait(barrier, 3)
@@ -661,33 +720,40 @@
     compute(1)
     pair_send(1)
     pair_wait(0)
-    go_up(0)
+    go_up(0, 0)
+    go_down(0, 1)
     compute(2)
     pair_send(2)
     pair_wait(1)
-    go_down(0)
+    go_down(0, 0)
+    go_down(1, 1)
     compute(3)
     pair_send(3)
     pair_wait(2)
-    go_up(1)
-    go_down(1)
-    go_up(2)
+    go_up(0, 1)
+    go_up(1, 0)
+    go_down(1, 0)
+    go_down(2, 1)
+    go_up(1, 1)
+    go_up(2, 0)
     pair_wait(3)
-    go_down(2)
-    go_up(3)
+    go_down(2, 0)
+    go_down(3, 1)
+    go_up(2, 1)
+    go_up(3, 0)
     for b in range(2):
         total = part(0, b)
-        down_copy(2, b).wait_recv()
-        total = total + rd[2, b].astype(F32)
-        up_copy(3, b).wait_recv()
-        grad[b * PART : (b + 1) * PART, :] = total + ru[3, b].astype(F32)
+        down_copy(DOWN[b] - 1, b).wait_recv()
+        total = total + rd[DOWN[b] - 1, b].astype(F32)
+        up_copy(UP[b] - 1, b).wait_recv()
+        grad[b * PART : (b + 1) * PART, :] = total + ru[UP[b] - 1, b].astype(F32)
     for n in range(4):
         for j in range(2):
             pair_copy(n, j).wait_send()
     for b in range(2):
-        for k in range(4):
+        for k in range(UP[b]):
             up_copy(k, b).wait_send()
-        for k in range(3):
+        for k in range(DOWN[b]):
             down_copy(k, b).wait_send()
 
 
@@ -700,18 +766,20 @@
         reduce_kernel,
         name="grad_reduce",
         out_shape=jax.ShapeDtypeStruct((SHARD, wide), F32),
-        in_specs=[hbm, vmem],
+        in_specs=[hbm, hbm],
         out_specs=vmem,
         scratch_shapes=[
+            pltpu.VMEM((GR, wide), BF16),
+            dma(()),
             pltpu.VMEM((4, GR, FC), BF16),
             pltpu.VMEM((4, FC, wide), F32),
             pltpu.VMEM((8, SHARD, wide), F32),
             pltpu.VMEM((4, 2, PART, wide), BF16),
             pltpu.VMEM((4, 2, PART, wide), BF16),
-            pltpu.VMEM((3, 2, PART, wide), BF16),
-            pltpu.VMEM((3, 2, PART, wide), BF16),
+            pltpu.VMEM((4, 2, PART, wide), BF16),
+            pltpu.VMEM((4, 2, PART, wide), BF16),
             dma((4,)), dma((4, 2)), dma((4, 2)),
-            dma((4, 2)), dma((4, 2)), dma((3, 2)), dma((3, 2)),
+            dma((4, 2)), dma((4, 2)), dma((4, 2)), dma((4, 2)),
         ],
         compiler_params=pltpu.CompilerParams(
             collective_id=1, has_side_effects=True, vmem_limit_bytes=VMEM_LIMIT

time: 146 us -> 140 us (0.959)
  Pallas kernels: 143 us -> 138 us
    pallas_call x1, Pallas kernels: 36.1 us -> 28.6 us  [reduce_call(): pl.pallas_call(reduce_kernel, name='grad_reduce', out_shape=jax.ShapeDtyp...]
    pallas_call x1, Pallas kernels: 15 us -> 18.9 us  [attention_call(): pl.pallas_call(attention_kernel, name='attention', out_shape=(jax.ShapeDt...]
    pallas_call x1, Pallas kernels: 91.6 us -> 90.1 us  [gather_call(): pl.pallas_call(gather_kernel, name='gather_project', out_shape=(jax.Shape...]
where the time goes in v3:
time: 140 us
  Pallas kernels  138 us (99%)
  local copies, waits for them, and re-layouts  1.65 us (1%)
    pallas_call x1, Pallas kernels, gather_call(): pl.pallas_call(gather_kernel, name='gather_project', out_shape=(jax.Shape...  90.1 us
    pallas_call x1, Pallas kernels, reduce_call(): pl.pallas_call(reduce_kernel, name='grad_reduce', out_shape=jax.ShapeDtyp...  28.6 us
    pallas_call x1, Pallas kernels, attention_call(): pl.pallas_call(attention_kernel, name='attention', out_shape=(jax.ShapeDt...  18.9 us

profile of v3, /device:TPU:2, one launch (start us, length us, event | category | flops | bytes accessed | tf_op | source)
XLA Modules:
  0.0 139.9 jit_solution(7533666590380311307)
XLA Ops:
  0.6 90.1 %gather_project.1 = (bf16[2048,2560]{1,0:T(8,128)(2,1)}, f32[2048,384]{1,0:T(8,128)}, bf16[2048,128]{1,0:T(8,128)(2,1)}) custom-call(s32[8,16]{1,0:T(8,128)} %bitcast.3, s32[8,16]{1,0:T(8,128)} %bitcast.7, s32[4,2,16]{2,1,0:T(2,128)} %bitcast.5, bf16[128,2560]{1,0:T(8,128)(2,1)} %tok_in.1, f32[4,8,2560]{2,1,0:T(8,128)} %mod_in.1, bf16[160,384]{1,0:T(8,128)(2,1)} %w.1, ...), custom_call_target="tpu_custom_call" | custom-call | tf_op jit(solution)/shard_map/gather_project/pallas_call | solution.py:350
  90.7 18.9 %attention.1 = (bf16[2048,128]{1,0:T(8,128)(2,1)}, bf16[2048,384]{1,0:T(8,128)(2,1)}) custom-call(s32[8,16]{1,0:T(8,128)} %bitcast.4, s32[4,2,16]{2,1,0:T(2,128)} %bitcast.6, f32[2048,384]{1,0:T(8,128)} %get-tuple-element.7.proj_in, bf16[2048,128]{1,0:T(8,128)(2,1)} %get-tuple-element.8.up_in, f32[2,128]{1,0:T(2,128)} %gain.1), custom_call_target="tpu_custom_call" | custom-call | tf_op jit(solution)/shard_map/attention/pallas_call | solution.py:582
  109.6 28.6 %grad_reduce.1 = f32[160,384]{1,0:T(8,128)} custom-call(bf16[2048,2560]{1,0:T(8,128)(2,1)} %get-tuple-element.10.rows, bf16[2048,384]{1,0:T(8,128)(2,1)} %get-tuple-element.11.hg_in), custom_call_target="tpu_custom_call" | custom-call | tf_op jit(solution)/shard_map/grad_reduce/pallas_call | solution.py:765
  138.2 1.7 %copy.11 = f32[160,384]{1,0:T(8,128)} copy(f32[160,384]{1,0:T(8,128)} %grad_reduce.1) | data formatting | bytes 491520

commit v4 on v3

--- a/solution.py
+++ b/solution.py
@@ -310,10 +310,8 @@
                 run(t)
         if n < CHUNKS:
             send_m2(n)
-        if n == 0:
-            send_m1(1)
-        if n + 2 < CHUNKS:
-            send_m1(n + 2)
+        if n + 1 < CHUNKS:
+            send_m1(n + 1)
         if n <= 4:
             weights(n)
         if n == 5:

time: 140 us -> 139 us (level)
  Pallas kernels: 138 us -> 136 us
    pallas_call x1, Pallas kernels: 28.6 us -> 30.9 us  [reduce_call(): pl.pallas_call(reduce_kernel, name='grad_reduce', out_shape=jax.ShapeDtyp...]
    pallas_call x1, Pallas kernels: 90.1 us -> 87.8 us  [gather_call(): pl.pallas_call(gather_kernel, name='gather_project', out_shape=(jax.Shape...]
    pallas_call x1, Pallas kernels: 18.9 us -> 16.8 us  [attention_call(): pl.pallas_call(attention_kernel, name='attention', out_shape=(jax.ShapeDt...]
where the time goes in v4:
time: 139 us; the launch traced here: 138 us
  Pallas kernels  136 us (98%)
  local copies, waits for them, and re-layouts  1.65 us (1%)
    pallas_call x1, Pallas kernels, gather_call(): pl.pallas_call(gather_kernel, name='gather_project', out_shape=(jax.Shape...  87.8 us
    pallas_call x1, Pallas kernels, reduce_call(): pl.pallas_call(reduce_kernel, name='grad_reduce', out_shape=jax.ShapeDtyp...  30.9 us
    pallas_call x1, Pallas kernels, attention_call(): pl.pallas_call(attention_kernel, name='attention', out_shape=(jax.ShapeDt...  16.8 us

profile of v4, /device:TPU:2, one launch (start us, length us, event | category | flops | bytes accessed | tf_op | source)
XLA Modules:
  0.0 137.9 jit_solution(11987621642794239908)
XLA Ops:
  0.6 87.8 %gather_project.1 = (bf16[2048,2560]{1,0:T(8,128)(2,1)}, f32[2048,384]{1,0:T(8,128)}, bf16[2048,128]{1,0:T(8,128)(2,1)}) custom-call(s32[8,16]{1,0:T(8,128)} %bitcast.3, s32[8,16]{1,0:T(8,128)} %bitcast.7, s32[4,2,16]{2,1,0:T(2,128)} %bitcast.5, bf16[128,2560]{1,0:T(8,128)(2,1)} %tok_in.1, f32[4,8,2560]{2,1,0:T(8,128)} %mod_in.1, bf16[160,384]{1,0:T(8,128)(2,1)} %w.1, ...), custom_call_target="tpu_custom_call" | custom-call | tf_op jit(solution)/shard_map/gather_project/pallas_call | solution.py:348
  88.4 16.8 %attention.1 = (bf16[2048,128]{1,0:T(8,128)(2,1)}, bf16[2048,384]{1,0:T(8,128)(2,1)}) custom-call(s32[8,16]{1,0:T(8,128)} %bitcast.4, s32[4,2,16]{2,1,0:T(2,128)} %bitcast.6, f32[2048,384]{1,0:T(8,128)} %get-tuple-element.7.proj_in, bf16[2048,128]{1,0:T(8,128)(2,1)} %get-tuple-element.8.up_in, f32[2,128]{1,0:T(2,128)} %gain.1), custom_call_target="tpu_custom_call" | custom-call | tf_op jit(solution)/shard_map/attention/pallas_call | solution.py:580
  105.3 30.9 %grad_reduce.1 = f32[160,384]{1,0:T(8,128)} custom-call(bf16[2048,2560]{1,0:T(8,128)(2,1)} %get-tuple-element.10.rows, bf16[2048,384]{1,0:T(8,128)(2,1)} %get-tuple-element.11.hg_in), custom_call_target="tpu_custom_call" | custom-call | tf_op jit(solution)/shard_map/grad_reduce/pallas_call | solution.py:763
  136.2 1.7 %copy.11 = f32[160,384]{1,0:T(8,128)} copy(f32[160,384]{1,0:T(8,128)} %grad_reduce.1) | data formatting | bytes 491520
